TPU v7x, 512 devices: a whole 4x4x16 slice. The times are simulated.
512 devices in a mesh: prefix: 8 (over x, core), branch: 32 (over z_lo, y), tensor: 2 (over z_hi).
Axes of the slice: x: 4, y: 4, z: 16 (z_hi: 2, z_lo: 8; z = z_hi * 8 + z_lo), core: 2. Of those that a mesh axis runs over, the one named last changes fastest.
Arguments:
- queries: bfloat16 [256, 128, 2048], P(('prefix', 'branch'), None, 'tensor'), may hold values from -16 to 16
- branch_keys: bfloat16 [256, 128, 512], P(('prefix', 'branch'), None, 'tensor'), may hold values from -4.5 to 4.5
- branch_values: bfloat16 [256, 128, 512], P(('prefix', 'branch'), None, 'tensor'), may hold values from -4.5 to 4.5
- grad_out: bfloat16 [256, 128, 2048], P(('prefix', 'branch'), None, 'tensor'), may hold values from -4.5 to 4.5
- prefix_keys: bfloat16 [2, 1024, 512], P(None, 'prefix', 'tensor'), may hold values from -16 to 16
- prefix_values: bfloat16 [2, 1024, 512], P(None, 'prefix', 'tensor'), may hold values from -4.5 to 4.5
- branch_prefix: int32 [256], P(('prefix', 'branch')), may hold values from 0 to 1
- branch_blocks: int32 [256], P(('prefix', 'branch')), may hold values from 1 to 1, as said below
Outputs:
- grad_queries: bfloat16 [256, 128, 2048], P(('prefix', 'branch'), None, 'tensor')
- grad_branch_keys: bfloat16 [256, 128, 512], P(('prefix', 'branch'), None, 'tensor')
- grad_branch_values: bfloat16 [256, 128, 512], P(('prefix', 'branch'), None, 'tensor')
- grad_prefix_keys: bfloat16 [2, 1024, 512], P(None, 'prefix', 'tensor')
- grad_prefix_values: bfloat16 [2, 1024, 512], P(None, 'prefix', 'tensor')
Inputs may be any that keep to these rules, and one draw needn't show every extreme that they name: Branch b continues prefix branch_prefix[b]. Branch b has 128 * branch_blocks[b] live tokens; some branch has the one block.
All inputs are finite; a program needn't handle non-finite values.
Results may differ from a plain program's by a relative error of at most 0.012.
The roundings to bfloat16 on the way count: a program that leaves them out, or rounds other values in their place, can miss the bound.
Values may be sent and summed in bfloat16 or wider, within the bound.
A program may use at most 64 MiB of HBM per device.

v0:
```python
import math

import jax
import jax.numpy as jnp
from jax import lax
from jax.sharding import PartitionSpec as P

HDIM = 128
BLK = 128


def head_columns(rows, head_index):
    return rows[:, head_index * HDIM : (head_index + 1) * HDIM]


def body(
    queries,
    branch_keys,
    branch_values,
    grad_out,
    prefix_keys,
    prefix_values,
    branch_prefix,
    branch_blocks,
):
    query_rows = queries[0]
    branch_rows = query_rows.shape[0]
    query_width = query_rows.shape[1]
    kv_width = branch_keys.shape[2]
    heads_here = query_width // HDIM
    kv_here = kv_width // HDIM
    group_size = heads_here // kv_here
    score_scale = 1.0 / math.sqrt(HDIM)
    whole_keys, whole_values = (
        lax.all_gather(prefix_keys, "prefix", axis=1, tiled=True),
        lax.all_gather(prefix_values, "prefix", axis=1, tiled=True),
    )
    prefix_count = whole_keys.shape[0]
    prefix_len = whole_keys.shape[1]
    prefix_owner = branch_prefix[0]
    key_rows = jnp.concatenate(
        [lax.dynamic_index_in_dim(whole_keys, prefix_owner, 0, keepdims=False), branch_keys[0]],
        axis=0,
    )
    value_rows = jnp.concatenate(
        [lax.dynamic_index_in_dim(whole_values, prefix_owner, 0, keepdims=False), branch_values[0]],
        axis=0,
    )
    key_total = key_rows.shape[0]
    positions = jnp.arange(branch_rows)
    columns = jnp.arange(key_total)
    allowed = (columns[None, :] < prefix_len) | (
        columns[None, :] - prefix_len <= positions[:, None]
    )
    allowed_pair = jnp.concatenate([allowed, allowed], axis=0)
    live_rows = positions < branch_blocks[0] * BLK
    grad_rows = jnp.where(live_rows[:, None], grad_out[0], jnp.zeros_like(grad_out[0]))
    query_parts = []
    key_parts = []
    value_parts = []
    for kv_index in range(kv_here):
        key_head = head_columns(key_rows, kv_index)
        value_head = head_columns(value_rows, kv_index)
        key_acc = jnp.zeros((key_total, HDIM), jnp.float32)
        value_acc = jnp.zeros((key_total, HDIM), jnp.float32)
        for pair_index in range(group_size // 2):
            first_head = kv_index * group_size + 2 * pair_index
            query_pair = jnp.concatenate(
                [head_columns(query_rows, first_head), head_columns(query_rows, first_head + 1)],
                axis=0,
            )
            grad_pair = jnp.concatenate(
                [head_columns(grad_rows, first_head), head_columns(grad_rows, first_head + 1)],
                axis=0,
            )
            scores = (
                jnp.einsum("rd,kd->rk", query_pair, key_head, preferred_element_type=jnp.float32)
                * score_scale
            )
            scores = jnp.where(allowed_pair, scores, -1e30)
            row_peak = jnp.max(scores, axis=1, keepdims=True)
            log_total = row_peak + jnp.log(
                jnp.sum(jnp.exp(scores - row_peak), axis=1, keepdims=True)
            )
            attention = jnp.exp(scores - log_total)
            attention_low = attention.astype(jnp.bfloat16)
            output = jnp.dot(attention_low, value_head, preferred_element_type=jnp.float32)
            row_delta = jnp.sum(grad_pair.astype(jnp.float32) * output, axis=1, keepdims=True)
            grad_attention = jnp.einsum(
                "rd,kd->rk", grad_pair, value_head, preferred_element_type=jnp.float32
            )
            grad_scores = (attention * (grad_attention - row_delta)).astype(jnp.bfloat16)
            grad_query = (
                jnp.dot(grad_scores, key_head, preferred_element_type=jnp.float32) * score_scale
            ).astype(jnp.bfloat16)
            query_parts.append(grad_query[:branch_rows])
            query_parts.append(grad_query[branch_rows:])
            key_acc = (
                key_acc
                + jnp.einsum(
                    "rk,rd->kd", grad_scores, query_pair, preferred_element_type=jnp.float32
                )
                * score_scale
            )
            value_acc = value_acc + jnp.einsum(
                "rk,rd->kd", attention_low, grad_pair, preferred_element_type=jnp.float32
            )
        key_parts.append(key_acc)
        value_parts.append(value_acc)
    grad_queries = jnp.concatenate(query_parts, axis=1)[None]
    key_grads = jnp.concatenate(key_parts, axis=1)
    value_grads = jnp.concatenate(value_parts, axis=1)
    grad_branch_keys = key_grads[prefix_len:].astype(jnp.bfloat16)[None]
    grad_branch_values = value_grads[prefix_len:].astype(jnp.bfloat16)[None]
    stacked = jnp.concatenate([key_grads[:prefix_len], value_grads[:prefix_len]], axis=1)
    chosen = (jnp.arange(prefix_count) == prefix_owner)[:, None, None]
    grad_term = jnp.where(chosen, stacked[None], 0.0)
    grad_share = lax.psum_scatter(
        grad_term, ("prefix", "branch"), scatter_dimension=1, tiled=True
    ).astype(jnp.bfloat16)
    summed = lax.all_gather(grad_share, "branch", axis=1, tiled=True)
    return (
        grad_queries,
        grad_branch_keys,
        grad_branch_values,
        summed[:, :, :kv_width],
        summed[:, :, kv_width:],
    )


def solution(mesh):
    placed = (
        P(("prefix", "branch"), None, "tensor"),
        P(("prefix", "branch"), None, "tensor"),
        P(("prefix", "branch"), None, "tensor"),
        P(("prefix", "branch"), None, "tensor"),
        P(None, "prefix", "tensor"),
        P(None, "prefix", "tensor"),
        P(("prefix", "branch")),
        P(("prefix", "branch")),
    )
    return jax.shard_map(
        body,
        mesh=mesh,
        in_specs=placed,
        out_specs=(
            P(("prefix", "branch"), None, "tensor"),
            P(("prefix", "branch"), None, "tensor"),
            P(("prefix", "branch"), None, "tensor"),
            P(None, "prefix", "tensor"),
            P(None, "prefix", "tensor"),
        ),
        check_vma=False,
    )
```

profile of v0, /device:TPU:8, one launch (start us, length us, event | category | flops | bytes accessed | tf_op | source)
XLA Modules:
  0.0 2209.3 jit_solution(1196615295989277122)
XLA Ops:
  7.2 0.0 all-gather.5.cloned.1.call-start
  7.2 0.7 all-gather.5.cloned.1.call-update
  7.9 0.0 all-gather.3.cloned.1.call-start
  7.9 0.7 all-gather.3.cloned.1.call-update
  9.3 1.1 copy.18
  11.1 1.3 dynamic-slice
  13.1 0.9 fusion.66
  14.0 0.0 copy-start
  14.1 0.1 fusion.27
  14.2 31.4 %all-gather.5.cloned.1.call-done = bf16[2,1024,256]{2,1,0:T(8,128)(2,1)} async-done(((bf16[2,128,256]{2,1,0:T(8,128)(2,1)}), bf16[2,1024,256]{2,1,0:T(8,128)(2,1)}) %all-gather.5.cloned.1.call-update) | async-done | bytes 1048592 | tf_op jit(solution)/shard_map/all_gather | solution.py:36
  45.6 33.1 %all-gather.3.cloned.1.call-done = bf16[2,1024,256]{2,1,0:T(8,128)(2,1)} async-done(((bf16[2,128,256]{2,1,0:T(8,128)(2,1)}), bf16[2,1024,256]{2,1,0:T(8,128)(2,1)}) %all-gather.3.cloned.1.call-update) | async-done | bytes 1048592 | tf_op jit(solution)/shard_map/all_gather | solution.py:35
  78.7 1.3 dynamic-slice_bitcast_fusion
  80.0 0.0 copy-done
  80.0 0.0 copy-start.1
  80.0 0.5 fusion.69
  80.5 0.3 exponential_reduce_fusion.1
  80.8 0.0 copy-done.1
  80.9 0.4 fusion.21
  81.3 0.4 fusion.9
  81.8 0.3 fusion.17
  82.1 0.3 fusion.36
  82.4 0.5 fusion.67
  82.9 0.3 exponential_reduce_fusion.3
  83.2 0.4 fusion.19
  83.6 0.4 fusion.11
  84.1 0.3 fusion.15
  84.4 0.3 fusion.37
  84.7 0.4 fusion.38
  85.1 0.4 fusion.39
  85.5 0.5 fusion.68
  86.0 0.3 exponential_reduce_fusion.2
  86.4 0.4 fusion.20
  86.8 0.4 fusion.10
  87.2 0.3 fusion.16
  87.6 0.5 fusion.70
  88.0 0.3 exponential_reduce_fusion
  88.4 0.4 fusion.22
  88.8 0.4 fusion.8
  89.2 0.3 fusion.18
  89.6 0.3 fusion.12
  89.9 0.3 fusion.13
  90.2 0.4 convolution_add_fusion
  90.6 0.4 convolution_add_fusion.1
  91.0 1.6 fusion.14
  92.8 0.9 copy.21
  93.6 0.7 copy.22
  94.4 0.7 copy.23
  95.1 1.9 copy.19
  97.1 2.6 broadcast_select_fusion
  99.7 1976.5 %all-reduce.2 = bf16[2,1024,512]{2,1,0:T(8,128)(2,1)S(1)} all-reduce(f32[2,1024,512]{2,1,0:T(8,128)} %broadcast_select_fusion), channel_id=2, replica_groups=mesh['prefix'=8,'branch'=32,'tensor'=2] {'prefix','branch'}, use_global_device_ids=true, to_apply=%region_12.13.clone | all-reduce | flops 1048576 | bytes 6291456
  2076.3 124.7 %all_gather.11 = bf16[2,128,512]{2,0,1:T(2,128)(2,1)S(1)} all-gather(bf16[2,4,512]{2,0,1:T(2,128)(2,1)S(1)} %copy.20), channel_id=1, replica_groups=mesh['prefix'=8,'branch'=32,'tensor'=2] {'branch'}, dimensions={1}, use_global_device_ids=true | all-gather | bytes 270336 | tf_op jit(solution)/shard_map/all_gather | solution.py:121
  2201.0 0.2 fusion.64
  2201.2 0.7 copy.24
  2201.8 0.7 copy.25
  (24 shorter events, 0.3 us)
Async XLA Ops:
  7.2 38.4 %all-gather.5.cloned.1.call-start = ((), (), s32[]{:S(2)}) async-start(), calls=%async_computation.1 | async-start | bytes 1179648 | tf_op jit(solution)/shard_map/all_gather | solution.py:36
  7.9 70.8 %all-gather.3.cloned.1.call-start = ((), (), s32[]{:S(2)}) async-start(), calls=%async_computation | async-start | bytes 1179648 | tf_op jit(solution)/shard_map/all_gather | solution.py:35
  14.0 65.9 %copy-start = (bf16[1,128,256]{2,1,0:T(8,128)(2,1)S(1)}, bf16[1,128,256]{2,1,0:T(8,128)(2,1)}, u32[]{:S(2)}) copy-start(bf16[1,128,256]{2,1,0:T(8,128)(2,1)} %param.9) | copy-start | bytes 196612
  80.0 0.8 copy-start.1
Sparse Core Ops, SparseCore 0:
  10.1 35.3 all-gather.4
  47.7 30.9 all-gather.2
where the time goes:
time: 2210 us
  blocking collectives  2100 us (95%)
  waiting for transfers between devices  65.9 us (3%)
    unnamed x1, blocking collectives  1980 us
    all_gather x1, blocking collectives, body(): summed = lax.all_gather(grad_share, 'branch', axis=1, tiled=True)  125 us
  transfers between devices with their start and end apart: 2, of which 2 were waited for; matrix products, arithmetic and copies ran while one was open for 0% of the time, Pallas kernels for 0%

commit v1 on v0

v1 whole, which is shorter than its diff:
```python
import math

import jax
import jax.numpy as jnp
from jax import lax
from jax.experimental import pallas as pl
from jax.experimental.pallas import tpu as pltpu
from jax.sharding import PartitionSpec as P

HDIM = 128
BLK = 128
NX = 4
NY = 4
NZ = 8
OWNERS = 2 * NX
GROUP = 4
SCALE = 1.0 / math.sqrt(HDIM)
SCALE2 = SCALE * math.log2(math.e)
MESH = pl.DeviceIdType.MESH

RELS = [(2, 0), (2, 1), (1, 0), (1, 1), (3, 0), (3, 1), (0, 1)]


def nt(a, b):
    return lax.dot_general(a, b, (((1,), (1,)), ((), ())), preferred_element_type=jnp.float32)


def tn(a, b):
    return lax.dot_general(a, b, (((0,), (0,)), ((), ())), preferred_element_type=jnp.float32)


def nn(a, b):
    return lax.dot_general(a, b, (((1,), (0,)), ((), ())), preferred_element_type=jnp.float32)


def fold(a, op):
    return op(a.reshape(a.shape[0] // 8, 8, a.shape[1]), axis=0)


def kernel(
    bp_ref,
    bb_ref,
    q_ref,
    bk_ref,
    bv_ref,
    do_ref,
    pk_ref,
    pv_ref,
    gq_ref,
    gbk_ref,
    gbv_ref,
    gpk_ref,
    gpv_ref,
    kv,
    keys,
    qs,
    dos,
    s_buf,
    dp_buf,
    p_buf,
    ds_buf,
    own,
    term,
    got,
    acc,
    ys,
    yr,
    zs,
    zr,
    fin,
    g_s,
    g_r,
    c_s,
    c_r,
    t_s,
    t_r,
    y_s,
    y_r,
    z_s,
    z_r,
    za_s,
    za_r,
    ya_s,
    ya_r,
):
    me = lax.axis_index("prefix")
    b = lax.axis_index("branch")
    x, c = me // 2, lax.rem(me, 2)
    z, y = b // NY, lax.rem(b, NY)

    def owner(dx, dc):
        return lax.rem(x - dx + NX, NX) * 2 + lax.rem(c + dc, 2)

    def at_owner(o):
        return {"prefix": o, "branch": b}

    def at_y(dy):
        return {"prefix": me, "branch": z * NY + lax.rem(y + dy, NY)}

    def at_z(dz):
        return {"prefix": me, "branch": lax.rem(z + dz, NZ) * NY + y}

    def send(src, dst, ss, rs, dev):
        cp = pltpu.make_async_remote_copy(
            src_ref=src, dst_ref=dst, send_sem=ss, recv_sem=rs, device_id=dev, device_id_type=MESH
        )
        cp.start()
        return cp

    barrier = pltpu.get_barrier_semaphore()
    peers = [at_owner(owner(dx, dc)) for dx, dc in RELS]
    peers += [at_y(d) for d in range(1, NY)] + [at_z(d) for d in range(1, NZ)]
    for dev in peers:
        pl.semaphore_signal(barrier, inc=1, device_id=dev, device_id_type=MESH)

    pid = bp_ref[0]
    rows = lax.broadcasted_iota(jnp.int32, (BLK, HDIM), 0)
    live = rows < bb_ref[0] * BLK
    for g in range(2):
        cols = pl.ds(g * HDIM, HDIM)
        kv[g, me, 0] = pk_ref[:, :, cols]
        kv[g, me, 1] = pv_ref[:, :, cols]
        for h in range(GROUP):
            wide = pl.ds((g * GROUP + h) * HDIM, HDIM)
            qs[g, pl.ds(h * BLK, BLK)] = q_ref[0, :, wide]
            grad = do_ref[0, :, wide]
            dos[g, pl.ds(h * BLK, BLK)] = jnp.where(live, grad, jnp.zeros_like(grad))
    pl.semaphore_wait(barrier, len(peers))

    copies = []
    gather = {}
    for g in range(2):
        for dx in (1, 3, 2):
            to = lax.rem(x + dx, NX) * 2 + c
            gather[g, dx] = send(kv.at[g, me], kv.at[g, me], g_s.at[g, dx], g_r.at[g, dx], at_owner(to))
        gather[g, 0] = send(kv.at[g, me], kv.at[g, me], c_s.at[g, 0], c_r.at[g, 0], at_owner(owner(0, 1)))
    copies += gather.values()

    def chosen(g, o):
        pair = [jnp.where(pid == 0, kv[g, o, kind, 0], kv[g, o, kind, 1]) for kind in range(2)]
        keys[o] = pair[0]
        return pair

    def scores(g, slot, k, v, peak):
        s = nt(k, qs[g])
        if slot is None:
            slot = OWNERS
            key = lax.broadcasted_iota(jnp.int32, s.shape, 0)
            query = lax.rem(lax.broadcasted_iota(jnp.int32, s.shape, 1), BLK)
            s = jnp.where(key <= query, s, -1e30)
        s_buf[slot] = s
        dp_buf[slot] = nt(v, dos[g])
        top = fold(s, jnp.max)
        return top if peak is None else jnp.maximum(peak, top)

    terms = {}
    for g in range(2):
        cols = pl.ds(g * HDIM, HDIM)
        peak = scores(g, None, bk_ref[0, :, cols], bv_ref[0, :, cols], None)
        peak = scores(g, me, *chosen(g, me), peak)
        passed = {}
        for dx in (1, 3, 2):
            gather[g, dx].wait_recv()
            o = owner(dx, 0)
            passed[dx] = send(kv.at[g, o], kv.at[g, o], c_s.at[g, dx], c_r.at[g, dx], at_owner(owner(0, 1)))
            peak = scores(g, o, *chosen(g, o), peak)
        for dx in (0, 1, 3, 2):
            (passed[dx] if dx else gather[g, 0]).wait_recv()
            o = owner(dx, 1)
            peak = scores(g, o, *chosen(g, o), peak)
        for dx in (1, 3, 2):
            passed[dx].wait_send()
        top = jnp.max(peak, axis=0, keepdims=True) * SCALE2

        def exps(i, total):
            e = jnp.exp2(s_buf[i] * SCALE2 - top)
            s_buf[i] = e
            return total + fold(e, jnp.sum)

        width = GROUP * BLK
        total = lax.fori_loop(0, OWNERS + 1, exps, jnp.zeros((8, width), jnp.float32))
        share = 1.0 / jnp.sum(total, axis=0, keepdims=True)

        def probs(i, total):
            p = s_buf[i] * share
            low = p.astype(jnp.bfloat16)
            s_buf[i] = p
            p_buf[i] = low
            return total + fold(low.astype(jnp.float32) * dp_buf[i], jnp.sum)

        total = lax.fori_loop(0, OWNERS + 1, probs, jnp.zeros((8, width), jnp.float32))
        delta = jnp.sum(total, axis=0, keepdims=True)

        def grads(i):
            ds = (s_buf[i] * (dp_buf[i] - delta)).astype(jnp.bfloat16)
            ds_buf[i] = ds
            return nn(ds, qs[g]) * SCALE, nn(p_buf[i], dos[g])

        for k, (dx, dc) in enumerate(RELS):
            o = owner(dx, dc)
            dk, dv = grads(o)
            term[g, k, 0:BLK] = dk.astype(jnp.bfloat16)
            term[g, k, BLK : 2 * BLK] = dv.astype(jnp.bfloat16)
            term[g, k, 2 * BLK : 2 * BLK + 16] = jnp.full((16, HDIM), pid, jnp.int32).astype(
                jnp.float32
            ).astype(jnp.bfloat16)
            terms[g, k] = send(term.at[g, k], got.at[g, k], t_s.at[g, k], t_r.at[g, k], at_owner(o))
        dk, dv = grads(me)
        own[g, 0:BLK] = dk
        own[g, BLK : 2 * BLK] = dv
        dk, dv = grads(OWNERS)
        gbk_ref[0, :, cols] = dk.astype(jnp.bfloat16)
        gbv_ref[0, :, cols] = dv.astype(jnp.bfloat16)
        dq = tn(keys[...].reshape(OWNERS * BLK, HDIM), ds_buf[0:OWNERS].reshape(OWNERS * BLK, width))
        dq = (dq + tn(bk_ref[0, :, cols], ds_buf[OWNERS])) * SCALE
        for h in range(GROUP):
            wide = pl.ds((g * GROUP + h) * HDIM, HDIM)
            gq_ref[0, :, wide] = dq[:, h * BLK : (h + 1) * BLK].T.astype(jnp.bfloat16)
    copies_sent = list(terms.values())

    along_y = {}
    for g in range(2):
        for k in range(len(RELS)):
            terms[g, k].wait_recv()
        for half in range(2):
            part = pl.ds(half * BLK, BLK)
            mine = own[g, part]
            sums = [jnp.where(pid == p, mine, 0.0) for p in range(2)]
            for k in range(len(RELS)):
                t = got[g, k, part].astype(jnp.float32)
                whose = got[g, k, 2 * BLK : 2 * BLK + 16].astype(jnp.float32)[0:1]
                first = jnp.broadcast_to(whose, t.shape) < 0.5
                sums[0] += jnp.where(first, t, 0.0)
                sums[1] += jnp.where(first, 0.0, t)
            for p in range(2):
                acc[g, p, half] = sums[p]
                for quarter in range(NY):
                    at = quarter * 32
                    ys[g, quarter, p, half] = sums[p][at : at + 32].astype(jnp.bfloat16)
        for dy in range(1, NY):
            along_y[g, dy] = send(
                ys.at[g, lax.rem(y + dy, NY)], yr.at[g, dy], y_s.at[g, dy], y_r.at[g, dy], at_y(dy)
            )
    copies_sent += along_y.values()

    along_z = {}
    for g in range(2):
        for dy in range(1, NY):
            along_y[g, dy].wait_recv()
        for p in range(2):
            for half in range(2):
                total = acc[g, p, half, pl.ds(y * 32, 32)]
                for dy in range(1, NY):
                    total += yr[g, dy, p, half].astype(jnp.float32)
                zs[g, 4 * p + 2 * half] = total[0:16]
                zs[g, 4 * p + 2 * half + 1] = total[16:32]
        for dz in range(1, NZ):
            along_z[g, dz] = send(
                zs.at[g, lax.rem(z + dz, NZ)], zr.at[g, dz], z_s.at[g, dz], z_r.at[g, dz], at_z(dz)
            )
    copies_sent += along_z.values()

    back_z = {}
    for g in range(2):
        total = zs[g, z]
        for dz in range(1, NZ):
            along_z[g, dz].wait_recv()
            total += zr[g, dz]
        fin[g, y, z] = total.astype(jnp.bfloat16)
        for dz in range(1, NZ):
            here = fin.at[g, y, z]
            back_z[g, dz] = send(here, here, za_s.at[g, dz], za_r.at[g, dz], at_z(dz))
    copies_sent += back_z.values()

    back_y = {}
    for g in range(2):
        for dz in range(1, NZ):
            back_z[g, dz].wait_recv()
        for dy in range(1, NY):
            here = fin.at[g, y]
            back_y[g, dy] = send(here, here, ya_s.at[g, dy], ya_r.at[g, dy], at_y(dy))
    copies_sent += back_y.values()

    for g in range(2):
        cols = pl.ds(g * HDIM, HDIM)
        for dy in range(1, NY):
            back_y[g, dy].wait_recv()
        for quarter in range(NY):
            for p in range(2):
                for low in range(2):
                    at = pl.ds(quarter * 32 + low * 16, 16)
                    gpk_ref[p, at, cols] = fin[g, quarter, 4 * p + low]
                    gpv_ref[p, at, cols] = fin[g, quarter, 4 * p + 2 + low]
    for cp in copies + copies_sent:
        cp.wait_send()


def body(queries, branch_keys, branch_values, grad_out, prefix_keys, prefix_values, branch_prefix, branch_blocks):
    bf16, f32 = jnp.bfloat16, jnp.float32
    vmem = pl.BlockSpec(memory_space=pltpu.VMEM)
    smem = pl.BlockSpec(memory_space=pltpu.SMEM)
    width = GROUP * BLK
    dma = pltpu.SemaphoreType.DMA
    return pl.pallas_call(
        kernel,
        out_shape=[
            jax.ShapeDtypeStruct(a.shape, bf16)
            for a in (queries, branch_keys, branch_values, prefix_keys, prefix_values)
        ],
        in_specs=[smem, smem] + [vmem] * 6,
        out_specs=[vmem] * 5,
        scratch_shapes=[
            pltpu.VMEM((2, OWNERS, 2, 2, BLK, HDIM), bf16),
            pltpu.VMEM((OWNERS, BLK, HDIM), bf16),
            pltpu.VMEM((2, width, HDIM), bf16),
            pltpu.VMEM((2, width, HDIM), bf16),
            pltpu.VMEM((OWNERS + 1, BLK, width), f32),
            pltpu.VMEM((OWNERS + 1, BLK, width), f32),
            pltpu.VMEM((OWNERS + 1, BLK, width), bf16),
            pltpu.VMEM((OWNERS + 1, BLK, width), bf16),
            pltpu.VMEM((2, 2 * BLK, HDIM), f32),
            pltpu.VMEM((2, 7, 2 * BLK + 16, HDIM), bf16),
            pltpu.VMEM((2, 7, 2 * BLK + 16, HDIM), bf16),
            pltpu.VMEM((2, 2, 2, BLK, HDIM), f32),
            pltpu.VMEM((2, NY, 2, 2, 32, HDIM), bf16),
            pltpu.VMEM((2, NY, 2, 2, 32, HDIM), bf16),
            pltpu.VMEM((2, NZ, 16, HDIM), f32),
            pltpu.VMEM((2, NZ, 16, HDIM), f32),
            pltpu.VMEM((2, NY, NZ, 16, HDIM), bf16),
        ]
        + [dma((2, NX))] * 4
        + [dma((2, 7))] * 2
        + [dma((2, NY))] * 2
        + [dma((2, NZ))] * 4
        + [dma((2, NY))] * 2,
        compiler_params=pltpu.CompilerParams(
            collective_id=0, has_side_effects=True, vmem_limit_bytes=40 << 20
        ),
        name="attention_backward",
    )(branch_prefix, branch_blocks, queries, branch_keys, branch_values, grad_out, prefix_keys, prefix_values)


def solution(mesh):
    split = P(("prefix", "branch"), None, "tensor")
    rows = P(None, "prefix", "tensor")
    ids = P(("prefix", "branch"))
    return jax.shard_map(
        body,
        mesh=mesh,
        in_specs=(split, split, split, split, rows, rows, ids, ids),
        out_specs=(split, split, split, rows, rows),
        check_vma=False,
    )
```

time: 2210 us -> 73.3 us (0.03)
  the two profiles are of different devices: /device:TPU:8 before, /device:TPU:6 now
where the time goes in v1:
time: 73.3 us; the launch traced here: 72.5 us
  Pallas kernels  61.9 us (84%)
  local copies, waits for them, and re-layouts  8.65 us (12%)
  between operations  1.95 us (3%)
    pallas_call x1, Pallas kernels, body(): pl.pallas_call(kernel, out_shape=[jax.ShapeDtypeStruct(a.shape, bf16) for...  61.9 us
    unnamed x17, local copies, waits for them, and re-layouts  8.65 us

profile of v1, /device:TPU:6, one launch (start us, length us, event | category | flops | bytes accessed | tf_op | source)
XLA Modules:
  0.0 72.5 jit_solution(13040814355298291503)
XLA Ops:
  1.9 0.0 copy-start
  1.9 0.9 %copy-done = bf16[1,128,1024]{2,1,0:T(8,128)(2,1)S(1)} copy-done((bf16[1,128,1024]{2,1,0:T(8,128)(2,1)S(1)}, bf16[1,128,1024]{2,1,0:T(8,128)(2,1)}, u32[]{:S(2)}) %copy-start) | copy-done | bytes 262168
  2.9 0.0 copy-start.1
  2.9 0.9 %copy-done.1 = bf16[1,128,1024]{2,1,0:T(8,128)(2,1)S(1)} copy-done((bf16[1,128,1024]{2,1,0:T(8,128)(2,1)S(1)}, bf16[1,128,1024]{2,1,0:T(8,128)(2,1)}, u32[]{:S(2)}) %copy-start.1) | copy-done | bytes 262168
  3.8 0.0 copy-start.2
  3.8 0.9 %copy-done.2 = bf16[2,128,256]{2,1,0:T(8,128)(2,1)S(1)} copy-done((bf16[2,128,256]{2,1,0:T(8,128)(2,1)S(1)}, bf16[2,128,256]{2,1,0:T(8,128)(2,1)}, u32[]{:S(2)}) %copy-start.2) | copy-done | bytes 131096
  4.7 0.0 copy-start.3
  4.7 0.9 %copy-done.3 = bf16[2,128,256]{2,1,0:T(8,128)(2,1)S(1)} copy-done((bf16[2,128,256]{2,1,0:T(8,128)(2,1)S(1)}, bf16[2,128,256]{2,1,0:T(8,128)(2,1)}, u32[]{:S(2)}) %copy-start.3) | copy-done | bytes 131096
  5.6 0.0 copy-start.4
  5.6 0.8 %copy-done.4 = bf16[1,128,256]{2,1,0:T(8,128)(2,1)S(1)} copy-done((bf16[1,128,256]{2,1,0:T(8,128)(2,1)S(1)}, bf16[1,128,256]{2,1,0:T(8,128)(2,1)}, u32[]{:S(2)}) %copy-start.4) | copy-done | bytes 65560
  6.5 0.0 copy-start.5
  6.5 0.8 %copy-done.5 = bf16[1,128,256]{2,1,0:T(8,128)(2,1)S(1)} copy-done((bf16[1,128,256]{2,1,0:T(8,128)(2,1)S(1)}, bf16[1,128,256]{2,1,0:T(8,128)(2,1)}, u32[]{:S(2)}) %copy-start.5) | copy-done | bytes 65560
  7.3 61.9 %attention_backward.1 = (bf16[1,128,1024]{2,1,0:T(8,128)(2,1)S(1)}, bf16[1,128,256]{2,1,0:T(8,128)(2,1)S(1)}, bf16[1,128,256]{2,1,0:T(8,128)(2,1)S(1)}, bf16[2,1...) custom-call(s32[1]{0:T(128)S(6)} %copy.18.bp_ref, s32[1]{0:T(128)S(6)} %copy.19.bb_ref, ...), custom_call_target="tpu_custom_call" | custom-call | tf_op jit(solution)/shard_map/attention_backward/pallas_call | solution.py:304
  69.3 0.7 copy.20
  70.0 0.6 copy.21
  70.6 0.6 copy.22
  71.2 0.7 copy.23
  71.9 0.7 copy.24
Async XLA Ops:
  1.9 1.0 %copy-start = (bf16[1,128,1024]{2,1,0:T(8,128)(2,1)S(1)}, bf16[1,128,1024]{2,1,0:T(8,128)(2,1)}, u32[]{:S(2)}) copy-start(bf16[1,128,1024]{2,1,0:T(8,128)(2,1)} %q_ref.1) | copy-start | bytes 786436
  2.9 0.9 %copy-start.1 = (bf16[1,128,1024]{2,1,0:T(8,128)(2,1)S(1)}, bf16[1,128,1024]{2,1,0:T(8,128)(2,1)}, u32[]{:S(2)}) copy-start(bf16[1,128,1024]{2,1,0:T(8,128)(2,1)} %do_ref.1) | copy-start | bytes 786436
  3.8 0.9 %copy-start.2 = (bf16[2,128,256]{2,1,0:T(8,128)(2,1)S(1)}, bf16[2,128,256]{2,1,0:T(8,128)(2,1)}, u32[]{:S(2)}) copy-start(bf16[2,128,256]{2,1,0:T(8,128)(2,1)} %pk_ref.1) | copy-start | bytes 393220
  4.7 0.9 %copy-start.3 = (bf16[2,128,256]{2,1,0:T(8,128)(2,1)S(1)}, bf16[2,128,256]{2,1,0:T(8,128)(2,1)}, u32[]{:S(2)}) copy-start(bf16[2,128,256]{2,1,0:T(8,128)(2,1)} %pv_ref.1) | copy-start | bytes 393220
  5.6 0.8 %copy-start.4 = (bf16[1,128,256]{2,1,0:T(8,128)(2,1)S(1)}, bf16[1,128,256]{2,1,0:T(8,128)(2,1)}, u32[]{:S(2)}) copy-start(bf16[1,128,256]{2,1,0:T(8,128)(2,1)} %bk_ref.1) | copy-start | bytes 196612
  6.5 0.8 %copy-start.5 = (bf16[1,128,256]{2,1,0:T(8,128)(2,1)S(1)}, bf16[1,128,256]{2,1,0:T(8,128)(2,1)}, u32[]{:S(2)}) copy-start(bf16[1,128,256]{2,1,0:T(8,128)(2,1)} %bv_ref.1) | copy-start | bytes 196612

commit v2 on v1

--- a/solution.py
+++ b/solution.py
@@ -40,12 +40,21 @@
 def kernel(
     bp_ref,
     bb_ref,
+    q_hbm,
+    bk_hbm,
+    bv_hbm,
+    do_hbm,
+    pk_hbm,
+    pv_hbm,
+    gq_hbm,
+    gbk_hbm,
+    gbv_hbm,
+    gpk_hbm,
+    gpv_hbm,
     q_ref,
     bk_ref,
     bv_ref,
     do_ref,
-    pk_ref,
-    pv_ref,
     gq_ref,
     gbk_ref,
     gbv_ref,
@@ -82,6 +91,8 @@
     za_r,
     ya_s,
     ya_r,
+    in_s,
+    out_s,
 ):
     me = lax.axis_index("prefix")
     b = lax.axis_index("branch")
@@ -107,6 +118,23 @@
         cp.start()
         return cp
 
+    def local(src, dst, sem):
+        cp = pltpu.make_async_copy(src, dst, sem)
+        cp.start()
+        return cp
+
+    prefix_in = []
+    for g in range(2):
+        for kind, ref in enumerate((pk_hbm, pv_hbm)):
+            part = ref.at[:, :, pl.ds(g * HDIM, HDIM)]
+            prefix_in.append(local(part, kv.at[g, me, kind], in_s.at[2 * g + kind]))
+    branch_in = [
+        local(src, dst, in_s.at[4 + i])
+        for i, (src, dst) in enumerate(
+            ((bk_hbm, bk_ref), (bv_hbm, bv_ref), (q_hbm, q_ref), (do_hbm, do_ref))
+        )
+    ]
+
     barrier = pltpu.get_barrier_semaphore()
     peers = [at_owner(owner(dx, dc)) for dx, dc in RELS]
     peers += [at_y(d) for d in range(1, NY)] + [at_z(d) for d in range(1, NZ)]
@@ -114,27 +142,28 @@
         pl.semaphore_signal(barrier, inc=1, device_id=dev, device_id_type=MESH)
 
     pid = bp_ref[0]
-    rows = lax.broadcasted_iota(jnp.int32, (BLK, HDIM), 0)
-    live = rows < bb_ref[0] * BLK
-    for g in range(2):
-        cols = pl.ds(g * HDIM, HDIM)
-        kv[g, me, 0] = pk_ref[:, :, cols]
-        kv[g, me, 1] = pv_ref[:, :, cols]
+    for cp in prefix_in:
+        cp.wait()
+    pl.semaphore_wait(barrier, len(peers))
+
+    copies = []
+    gather = {}
+    for g in range(2):
+        for dx in (1, 3, 2):
+            to = lax.rem(x + dx, NX) * 2 + c
+            gather[g, dx] = send(kv.at[g, me], kv.at[g, me], g_s.at[g, dx], g_r.at[g, dx], at_owner(to))
+        gather[g, 0] = send(kv.at[g, me], kv.at[g, me], c_s.at[g, 0], c_r.at[g, 0], at_owner(owner(0, 1)))
+    copies += gather.values()
+
+    for cp in branch_in:
+        cp.wait()
+    live = lax.broadcasted_iota(jnp.int32, (BLK, HDIM), 0) < bb_ref[0] * BLK
+    for g in range(2):
         for h in range(GROUP):
             wide = pl.ds((g * GROUP + h) * HDIM, HDIM)
             qs[g, pl.ds(h * BLK, BLK)] = q_ref[0, :, wide]
             grad = do_ref[0, :, wide]
             dos[g, pl.ds(h * BLK, BLK)] = jnp.where(live, grad, jnp.zeros_like(grad))
-    pl.semaphore_wait(barrier, len(peers))
-
-    copies = []
-    gather = {}
-    for g in range(2):
-        for dx in (1, 3, 2):
-            to = lax.rem(x + dx, NX) * 2 + c
-            gather[g, dx] = send(kv.at[g, me], kv.at[g, me], g_s.at[g, dx], g_r.at[g, dx], at_owner(to))
-        gather[g, 0] = send(kv.at[g, me], kv.at[g, me], c_s.at[g, 0], c_r.at[g, 0], at_owner(owner(0, 1)))
-    copies += gather.values()
 
     def chosen(g, o):
         pair = [jnp.where(pid == 0, kv[g, o, kind, 0], kv[g, o, kind, 1]) for kind in range(2)]
@@ -216,6 +245,10 @@
         for h in range(GROUP):
             wide = pl.ds((g * GROUP + h) * HDIM, HDIM)
             gq_ref[0, :, wide] = dq[:, h * BLK : (h + 1) * BLK].T.astype(jnp.bfloat16)
+    outs = [
+        local(src, dst, out_s.at[i])
+        for i, (src, dst) in enumerate(((gq_ref, gq_hbm), (gbk_ref, gbk_hbm), (gbv_ref, gbv_hbm)))
+    ]
     copies_sent = list(terms.values())
 
     along_y = {}
@@ -291,25 +324,43 @@
                     at = pl.ds(quarter * 32 + low * 16, 16)
                     gpk_ref[p, at, cols] = fin[g, quarter, 4 * p + low]
                     gpv_ref[p, at, cols] = fin[g, quarter, 4 * p + 2 + low]
+    outs += [local(gpk_ref, gpk_hbm, out_s.at[3]), local(gpv_ref, gpv_hbm, out_s.at[4])]
     for cp in copies + copies_sent:
         cp.wait_send()
+    for cp in outs:
+        cp.wait()
+
+
+def hand_over(*refs):
+    for i in range(5):
+        refs[5 + i][...] = refs[i][...]
 
 
 def body(queries, branch_keys, branch_values, grad_out, prefix_keys, prefix_values, branch_prefix, branch_blocks):
     bf16, f32 = jnp.bfloat16, jnp.float32
-    vmem = pl.BlockSpec(memory_space=pltpu.VMEM)
     smem = pl.BlockSpec(memory_space=pltpu.SMEM)
+    hbm = pl.BlockSpec(memory_space=pltpu.HBM)
+    anywhere = pl.BlockSpec(memory_space=pl.ANY)
     width = GROUP * BLK
     dma = pltpu.SemaphoreType.DMA
-    return pl.pallas_call(
+    shapes = [a.shape for a in (queries, branch_keys, branch_values, prefix_keys, prefix_values)]
+    wide, narrow, _, prefix, _ = (pltpu.VMEM(shape, bf16) for shape in shapes)
+    out_shape = [jax.ShapeDtypeStruct(shape, bf16) for shape in shapes]
+    results = pl.pallas_call(
         kernel,
-        out_shape=[
-            jax.ShapeDtypeStruct(a.shape, bf16)
-            for a in (queries, branch_keys, branch_values, prefix_keys, prefix_values)
-        ],
-        in_specs=[smem, smem] + [vmem] * 6,
-        out_specs=[vmem] * 5,
+        out_shape=out_shape,
+        in_specs=[smem, smem] + [hbm] * 6,
+        out_specs=[anywhere] * 5,
         scratch_shapes=[
+            wide,
+            narrow,
+            narrow,
+            wide,
+            wide,
+            narrow,
+            narrow,
+            prefix,
+            prefix,
             pltpu.VMEM((2, OWNERS, 2, 2, BLK, HDIM), bf16),
             pltpu.VMEM((OWNERS, BLK, HDIM), bf16),
             pltpu.VMEM((2, width, HDIM), bf16),
@@ -332,12 +383,20 @@
         + [dma((2, 7))] * 2
         + [dma((2, NY))] * 2
         + [dma((2, NZ))] * 4
-        + [dma((2, NY))] * 2,
+        + [dma((2, NY))] * 2
+        + [dma((8,)), dma((5,))],
         compiler_params=pltpu.CompilerParams(
-            collective_id=0, has_side_effects=True, vmem_limit_bytes=40 << 20
+            collective_id=0, has_side_effects=True, vmem_limit_bytes=63 << 20
         ),
         name="attention_backward",
     )(branch_prefix, branch_blocks, queries, branch_keys, branch_values, grad_out, prefix_keys, prefix_values)
+    return pl.pallas_call(
+        hand_over,
+        out_shape=out_shape,
+        in_specs=[pl.BlockSpec(memory_space=pltpu.VMEM)] * 5,
+        out_specs=[pl.BlockSpec(memory_space=pltpu.VMEM)] * 5,
+        name="hand_over",
+    )(*results)
 
 
 def solution(mesh):

time: 73.3 us -> 67.2 us (0.917)
  local copies, waits for them, and re-layouts: 8.65 us -> 0 us
  Pallas kernels: 61.9 us -> 64.6 us
    unnamed x17 -> x0, local copies, waits for them, and re-layouts: 8.65 us -> none
    pallas_call x1 -> x2, Pallas kernels: 61.9 us -> 64.6 us  [the longest x1 62.7 us: body(): pl.pallas_call(kernel, out_shape=out_shape, in_specs=[smem, smem] + [hbm]...]
where the time goes in v2:
time: 67.2 us; the launch traced here: 66.6 us
  Pallas kernels  64.6 us (96%)
  between operations  1.93 us (3%)
    pallas_call x1, Pallas kernels, body(): pl.pallas_call(kernel, out_shape=out_shape, in_specs=[smem, smem] + [hbm]...  62.7 us
    pallas_call x1, Pallas kernels, body(): pl.pallas_call(hand_over, out_shape=out_shape, in_specs=[pl.BlockSpec(mem...  1.95 us

profile of v2, /device:TPU:6, one launch (start us, length us, event | category | flops | bytes accessed | tf_op | source)
XLA Modules:
  0.0 66.6 jit_solution(17191955843520883870)
XLA Ops:
  1.9 62.7 %attention_backward.1 = (bf16[1,128,1024]{2,1,0:T(8,128)(2,1)}, bf16[1,128,256]{2,1,0:T(8,128)(2,1)}, bf16[1,128,256]{2,1,0:T(8,128)(2,1)}, bf16[2,128,256]{2,1,0:T(8,128)(2,1)}, bf16[2,128,256]{2,1,0:T(8,128)(2,1)}) custom-call(s32[1]{0:T(128)S(6)} %copy.13.bp_ref, s32[1]{0:T(128)S(6)} %copy.14.bb_ref, bf16[1,128,1024]{2,1,0:T(8,128)(2,1)} %q_hbm.1, ...), custom_call_target="tpu_custom_call" | custom-call | tf_op jit(solution)/shard_map/attention_backward/pallas_call | solution.py:349
  64.6 2.0 %hand_over.1 = (bf16[1,128,1024]{2,1,0:T(8,128)(2,1)}, bf16[1,128,256]{2,1,0:T(8,128)(2,1)}, bf16[1,128,256]{2,1,0:T(8,128)(2,1)}, bf16[2,128,256]{2,1,0:T(8,128)(2,1)}, bf16[2,128,256]{2,1,0:T(8,128)(2,1)}) custom-call(bf16[1,128,1024]{2,1,0:T(8,128)(2,1)} %get-tuple-element.10.refs_0_, bf16[1,128,256]{2,1,0:T(8,128)(2,1)} %get-tuple-element.11.refs_1_, ...), custom_call_target="tpu_custom_call" | custom-call | tf_op jit(solution)/shard_map/hand_over/pallas_call | solution.py:393

commit v3 on v2

v3 whole, which is shorter than its diff:
```python
import math

import jax
import jax.numpy as jnp
from jax import lax
from jax.experimental import pallas as pl
from jax.experimental.pallas import tpu as pltpu
from jax.sharding import PartitionSpec as P

HDIM = 128
BLK = 128
NX = 4
NY = 4
NZ = 8
OWNERS = 2 * NX
GROUP = 4
SCALE = 1.0 / math.sqrt(HDIM)
SCALE2 = SCALE * math.log2(math.e)
MESH = pl.DeviceIdType.MESH

STEPS = (2, 1, 3)
RELS = [(d, dc) for d in STEPS for dc in range(2)] + [(0, 1)]
ROWS = BLK // NY


def nt(a, b):
    return lax.dot_general(a, b, (((1,), (1,)), ((), ())), preferred_element_type=jnp.float32)


def tn(a, b):
    return lax.dot_general(a, b, (((0,), (0,)), ((), ())), preferred_element_type=jnp.float32)


def nn(a, b):
    return lax.dot_general(a, b, (((1,), (0,)), ((), ())), preferred_element_type=jnp.float32)


def fold(a, op):
    return op(a.reshape(a.shape[0] // 8, 8, a.shape[1]), axis=0)


def kernel(
    bp_ref,
    bb_ref,
    q_hbm,
    bk_hbm,
    bv_hbm,
    do_hbm,
    pk_hbm,
    pv_hbm,
    gq_hbm,
    gbk_hbm,
    gbv_hbm,
    gpk_hbm,
    gpv_hbm,
    q_ref,
    bk_ref,
    bv_ref,
    do_ref,
    gq_ref,
    gbk_ref,
    gbv_ref,
    gpk_ref,
    gpv_ref,
    kva,
    kvb,
    keys,
    qs,
    dos,
    s_buf,
    dp_buf,
    p_buf,
    ds_buf,
    own,
    term,
    got,
    acc,
    ys,
    yr,
    zs,
    zr,
    fin,
    a_s,
    a_r,
    b_s,
    b_r,
    u_s,
    u_r,
    ca_s,
    ca_r,
    cb_s,
    cb_r,
    t_s,
    t_r,
    y_s,
    y_r,
    z_s,
    z_r,
    za_s,
    za_r,
    ya_s,
    ya_r,
    in_s,
    out_s,
):
    me = lax.axis_index("prefix")
    b = lax.axis_index("branch")
    x, c = me // 2, lax.rem(me, 2)
    z, y = b // NY, lax.rem(b, NY)

    def at(dx=0, dc=0, dy=0, dz=0):
        return {
            "prefix": lax.rem(x + dx + NX, NX) * 2 + lax.rem(c + dc, 2),
            "branch": lax.rem(z + dz, NZ) * NY + lax.rem(y + dy + NY, NY),
        }

    def send(src, dst, ss, rs, dev):
        cp = pltpu.make_async_remote_copy(
            src_ref=src, dst_ref=dst, send_sem=ss, recv_sem=rs, device_id=dev, device_id_type=MESH
        )
        cp.start()
        return cp

    def local(src, dst, sem):
        cp = pltpu.make_async_copy(src, dst, sem)
        cp.start()
        return cp

    prefix_in = []
    for kind, ref in enumerate((pk_hbm, pv_hbm)):
        for r in range(NY):
            at_row = pl.multiple_of(lax.rem(y - r + NY, NY) * ROWS, ROWS)
            part = ref.at[:, pl.ds(at_row, ROWS), pl.ds(HDIM, HDIM)]
            prefix_in.append(local(part, kvb.at[0, 0, r, kind], in_s.at[NY * kind + r]))
        part = ref.at[:, :, pl.ds(0, HDIM)]
        prefix_in.append(local(part, kva.at[0, 0, kind], in_s.at[2 * NY + kind]))
    branch_in = [
        local(src, dst, in_s.at[2 * NY + 2 + i])
        for i, (src, dst) in enumerate(
            ((bk_hbm, bk_ref), (bv_hbm, bv_ref), (q_hbm, q_ref), (do_hbm, do_ref))
        )
    ]

    barrier = pltpu.get_barrier_semaphore()
    peers = [at(dx=-d, dc=dc) for d, dc in RELS] + [at(dy=-d, dc=dc) for d, dc in RELS[:-1]]
    peers += [at(dz=d) for d in range(1, NZ)]
    for dev in peers:
        pl.semaphore_signal(barrier, inc=1, device_id=dev, device_id_type=MESH)

    pid = bp_ref[0]
    for cp in prefix_in:
        cp.wait()
    pl.semaphore_wait(barrier, len(peers))

    rest = pl.ds(1, NX - 1)
    first_b = [
        send(kvb.at[0, 0, 0], kvb.at[0, d, 0], b_s.at[d], b_r.at[d], at(dx=d)) for d in range(1, NX)
    ]
    first_a = {
        d: send(kva.at[0, 0], kva.at[0, d], a_s.at[d], a_r.at[d], at(dx=d)) for d in (1, 3, 2)
    }
    over_a = {0: send(kva.at[0, 0], kva.at[1, 0], ca_s.at[0], ca_r.at[0], at(dc=1))}
    over_b = {NY: send(kvb.at[0, 0], kvb.at[1, 0], cb_s.at[NY], cb_r.at[NY], at(dc=1))}

    for cp in branch_in:
        cp.wait()
    live = lax.broadcasted_iota(jnp.int32, (BLK, HDIM), 0) < bb_ref[0] * BLK
    for g in range(2):
        for h in range(GROUP):
            wide = pl.ds((g * GROUP + h) * HDIM, HDIM)
            qs[g, pl.ds(h * BLK, BLK)] = q_ref[0, :, wide]
            grad = do_ref[0, :, wide]
            dos[g, pl.ds(h * BLK, BLK)] = jnp.where(live, grad, jnp.zeros_like(grad))

    def scores(g, slot, k, v, peak=None):
        s = nt(k, qs[g])
        if slot == OWNERS:
            key = lax.broadcasted_iota(jnp.int32, s.shape, 0)
            query = lax.rem(lax.broadcasted_iota(jnp.int32, s.shape, 1), BLK)
            s = jnp.where(key <= query, s, -1e30)
        s_buf[g, slot] = s
        dp_buf[g, slot] = nt(v, dos[g])
        top = fold(s, jnp.max)
        return top if peak is None else jnp.maximum(peak, top)

    def prefix_scores(g, other, d, peak):
        if g == 0:
            pairs = [[kva[other, d, kind, p] for p in range(2)] for kind in range(2)]
        else:
            pairs = [
                [kvb[other, d, :, kind, p].reshape(BLK, HDIM) for p in range(2)] for kind in range(2)
            ]
        k, v = [jnp.where(pid == 0, pair[0], pair[1]) for pair in pairs]
        slot = other * NX + d
        keys[g, slot] = k
        return scores(g, slot, k, v, peak)

    def own_columns(g):
        return pl.ds(g * HDIM, HDIM)

    peaks = []
    for g in range(2):
        cols = own_columns(g)
        peaks.append(scores(g, OWNERS, bk_ref[0, :, cols], bv_ref[0, :, cols]))
        peaks[g] = prefix_scores(g, 0, 0, peaks[g])
    for cp in first_b:
        cp.wait_recv()
    mine = kvb.at[0, rest, 0]
    second_b = {d: send(mine, kvb.at[0, rest, d], u_s.at[d], u_r.at[d], at(dy=d)) for d in (1, 3, 2)}
    over_b[0] = send(mine, kvb.at[1, rest, 0], cb_s.at[0], cb_r.at[0], at(dc=1))
    for d in (1, 3, 2):
        first_a[d].wait_recv()
        over_a[d] = send(kva.at[0, d], kva.at[1, d], ca_s.at[d], ca_r.at[d], at(dc=1))
        peaks[0] = prefix_scores(0, 0, d, peaks[0])
    for d in (1, 3, 2):
        second_b[d].wait_recv()
        here, there = kvb.at[0, rest, d], kvb.at[1, rest, d]
        over_b[d] = send(here, there, cb_s.at[d], cb_r.at[d], at(dc=1))
    for d in (0, 1, 3, 2):
        over_a[d].wait_recv()
        peaks[0] = prefix_scores(0, 1, d, peaks[0])
    sent = first_b + list(first_a.values()) + list(over_a.values())
    sent += list(second_b.values()) + list(over_b.values())

    width = GROUP * BLK
    terms = {}
    for g in range(2):
        cols = own_columns(g)
        if g == 1:
            for d in (1, 3, 2):
                peaks[1] = prefix_scores(1, 0, d, peaks[1])
            for d in (NY, 0, 1, 3, 2):
                over_b[d].wait_recv()
            for d in range(NX):
                peaks[1] = prefix_scores(1, 1, d, peaks[1])
        top = jnp.max(peaks[g], axis=0, keepdims=True) * SCALE2

        def exps(i, total):
            e = jnp.exp2(s_buf[g, i] * SCALE2 - top)
            s_buf[g, i] = e
            return total + fold(e, jnp.sum)

        total = lax.fori_loop(0, OWNERS + 1, exps, jnp.zeros((8, width), jnp.float32))
        share = 1.0 / jnp.sum(total, axis=0, keepdims=True)

        def probs(i, total):
            p = s_buf[g, i] * share
            low = p.astype(jnp.bfloat16)
            s_buf[g, i] = p
            p_buf[g, i] = low
            return total + fold(low.astype(jnp.float32) * dp_buf[g, i], jnp.sum)

        total = lax.fori_loop(0, OWNERS + 1, probs, jnp.zeros((8, width), jnp.float32))
        delta = jnp.sum(total, axis=0, keepdims=True)

        def grads(i):
            ds = (s_buf[g, i] * (dp_buf[g, i] - delta)).astype(jnp.bfloat16)
            ds_buf[g, i] = ds
            return nn(ds, qs[g]) * SCALE, nn(p_buf[g, i], dos[g])

        whose = jnp.full((16, HDIM), pid, jnp.int32).astype(jnp.float32).astype(jnp.bfloat16)
        for k, (d, dc) in enumerate(RELS):
            term[g, k, 2 * BLK : 2 * BLK + 16] = whose
        if g == 0:
            for k, (d, dc) in enumerate(RELS):
                for kind, part in enumerate(grads(dc * NX + d)):
                    term[0, k, kind * BLK : (kind + 1) * BLK] = part.astype(jnp.bfloat16)
                terms[0, k] = send(term.at[0, k], got.at[0, k], t_s.at[0, k], t_r.at[0, k], at(dx=-d, dc=dc))
            for kind, part in enumerate(grads(0)):
                own[0, kind * BLK : (kind + 1) * BLK] = part
        else:
            for dc in range(2):
                for d in range(NX):
                    for kind, part in enumerate(grads(dc * NX + d)):
                        low = part.astype(jnp.bfloat16)
                        at_row = (2 * d + kind) * ROWS
                        for k, (r, other) in enumerate(RELS):
                            if other == dc:
                                term[1, k, at_row : at_row + ROWS] = low[r * ROWS : (r + 1) * ROWS]
                        if dc == 0:
                            own[1, at_row : at_row + ROWS] = part[0:ROWS]
                for k, (r, other) in enumerate(RELS):
                    if other == dc:
                        terms[1, k] = send(
                            term.at[1, k], got.at[1, k], t_s.at[1, k], t_r.at[1, k], at(dy=-r, dc=dc)
                        )
        for ref, part in zip((gbk_ref, gbv_ref), grads(OWNERS)):
            ref[0, :, cols] = part.astype(jnp.bfloat16)
    for g in range(2):
        cols = own_columns(g)
        dq = tn(keys[g].reshape(OWNERS * BLK, HDIM), ds_buf[g, 0:OWNERS].reshape(OWNERS * BLK, width))
        dq = (dq + tn(bk_ref[0, :, cols], ds_buf[g, OWNERS])) * SCALE
        for h in range(GROUP):
            wide = pl.ds((g * GROUP + h) * HDIM, HDIM)
            gq_ref[0, :, wide] = dq[:, h * BLK : (h + 1) * BLK].T.astype(jnp.bfloat16)
    outs = [
        local(src, dst, out_s.at[i])
        for i, (src, dst) in enumerate(((gq_ref, gq_hbm), (gbk_ref, gbk_hbm), (gbv_ref, gbv_hbm)))
    ]
    sent += terms.values()

    second = {}
    for g in range(2):
        for k in range(len(RELS)):
            terms[g, k].wait_recv()
        for block in range(2 * NY):
            part = pl.ds(block * ROWS, ROWS)
            here = own[g, part]
            sums = [jnp.where(pid == p, here, 0.0) for p in range(2)]
            for k in range(len(RELS)):
                t = got[g, k, part].astype(jnp.float32)
                whose = got[g, k, 2 * BLK : 2 * BLK + 16].astype(jnp.float32)[0:1]
                first = jnp.broadcast_to(whose, t.shape) < 0.5
                sums[0] += jnp.where(first, t, 0.0)
                sums[1] += jnp.where(first, 0.0, t)
            kind, quarter = (block // NY, block % NY) if g == 0 else (block % 2, block // 2)
            for p in range(2):
                acc[g, quarter, p, kind] = sums[p]
                ys[g, quarter, p, kind] = sums[p].astype(jnp.bfloat16)
        for d in range(1, NY):
            src, dev = (lax.rem(y + d, NY), at(dy=d)) if g == 0 else (d, at(dx=-d))
            second[g, d] = send(ys.at[g, src], yr.at[g, d], y_s.at[g, d], y_r.at[g, d], dev)
    sent += second.values()

    along_z = {}
    for g in range(2):
        for d in range(1, NY):
            second[g, d].wait_recv()
        for p in range(2):
            for kind in range(2):
                total = acc[g, y if g == 0 else 0, p, kind]
                for d in range(1, NY):
                    total += yr[g, d, p, kind].astype(jnp.float32)
                zs[g, 4 * p + 2 * kind] = total[0:16]
                zs[g, 4 * p + 2 * kind + 1] = total[16:32]
        for d in range(1, NZ):
            src = zs.at[g, lax.rem(z + d, NZ)]
            along_z[g, d] = send(src, zr.at[g, d], z_s.at[g, d], z_r.at[g, d], at(dz=d))
    sent += along_z.values()

    back_z = {}
    for g in range(2):
        total = zs[g, z]
        for d in range(1, NZ):
            along_z[g, d].wait_recv()
            total += zr[g, d]
        fin[g, y, z] = total.astype(jnp.bfloat16)
        for d in range(1, NZ):
            here = fin.at[g, y, z]
            back_z[g, d] = send(here, here, za_s.at[g, d], za_r.at[g, d], at(dz=d))
    sent += back_z.values()

    back_y = {}
    for g in range(2):
        for d in range(1, NZ):
            back_z[g, d].wait_recv()
        for d in range(1, NY):
            here = fin.at[g, y]
            back_y[g, d] = send(here, here, ya_s.at[g, d], ya_r.at[g, d], at(dy=d))
    sent += back_y.values()

    for g in range(2):
        cols = own_columns(g)
        for d in range(1, NY):
            back_y[g, d].wait_recv()
        for quarter in range(NY):
            for p in range(2):
                for low in range(2):
                    row = pl.ds(quarter * ROWS + low * 16, 16)
                    gpk_ref[p, row, cols] = fin[g, quarter, 4 * p + low]
                    gpv_ref[p, row, cols] = fin[g, quarter, 4 * p + 2 + low]
    outs += [local(gpk_ref, gpk_hbm, out_s.at[3]), local(gpv_ref, gpv_hbm, out_s.at[4])]
    for cp in sent:
        cp.wait_send()
    for cp in outs:
        cp.wait()


def hand_over(*refs):
    for i in range(5):
        refs[5 + i][...] = refs[i][...]


def body(queries, branch_keys, branch_values, grad_out, prefix_keys, prefix_values, branch_prefix, branch_blocks):
    bf16, f32 = jnp.bfloat16, jnp.float32
    smem = pl.BlockSpec(memory_space=pltpu.SMEM)
    hbm = pl.BlockSpec(memory_space=pltpu.HBM)
    anywhere = pl.BlockSpec(memory_space=pl.ANY)
    width = GROUP * BLK
    dma = pltpu.SemaphoreType.DMA
    shapes = [a.shape for a in (queries, branch_keys, branch_values, prefix_keys, prefix_values)]
    wide, narrow, _, prefix, _ = (pltpu.VMEM(shape, bf16) for shape in shapes)
    out_shape = [jax.ShapeDtypeStruct(shape, bf16) for shape in shapes]
    results = pl.pallas_call(
        kernel,
        out_shape=out_shape,
        in_specs=[smem, smem] + [hbm] * 6,
        out_specs=[anywhere] * 5,
        scratch_shapes=[
            wide,
            narrow,
            narrow,
            wide,
            wide,
            narrow,
            narrow,
            prefix,
            prefix,
            pltpu.VMEM((2, NX, 2, 2, BLK, HDIM), bf16),
            pltpu.VMEM((2, NX, NY, 2, 2, ROWS, HDIM), bf16),
            pltpu.VMEM((2, OWNERS, BLK, HDIM), bf16),
            pltpu.VMEM((2, width, HDIM), bf16),
            pltpu.VMEM((2, width, HDIM), bf16),
            pltpu.VMEM((2, OWNERS + 1, BLK, width), f32),
            pltpu.VMEM((2, OWNERS + 1, BLK, width), f32),
            pltpu.VMEM((2, OWNERS + 1, BLK, width), bf16),
            pltpu.VMEM((2, OWNERS + 1, BLK, width), bf16),
            pltpu.VMEM((2, 2 * BLK, HDIM), f32),
            pltpu.VMEM((2, len(RELS), 2 * BLK + 16, HDIM), bf16),
            pltpu.VMEM((2, len(RELS), 2 * BLK + 16, HDIM), bf16),
            pltpu.VMEM((2, NY, 2, 2, ROWS, HDIM), f32),
            pltpu.VMEM((2, NY, 2, 2, ROWS, HDIM), bf16),
            pltpu.VMEM((2, NY, 2, 2, ROWS, HDIM), bf16),
            pltpu.VMEM((2, NZ, 16, HDIM), f32),
            pltpu.VMEM((2, NZ, 16, HDIM), f32),
            pltpu.VMEM((2, NY, NZ, 16, HDIM), bf16),
        ]
        + [dma((NX,))] * 4
        + [dma((NY,))] * 2
        + [dma((NX,))] * 2
        + [dma((NY + 1,))] * 2
        + [dma((2, len(RELS)))] * 2
        + [dma((2, NY))] * 2
        + [dma((2, NZ))] * 4
        + [dma((2, NY))] * 2
        + [dma((2 * NY + 6,)), dma((5,))],
        compiler_params=pltpu.CompilerParams(
            collective_id=0, has_side_effects=True, vmem_limit_bytes=63 << 20
        ),
        name="attention_backward",
    )(branch_prefix, branch_blocks, queries, branch_keys, branch_values, grad_out, prefix_keys, prefix_values)
    return pl.pallas_call(
        hand_over,
        out_shape=out_shape,
        in_specs=[pl.BlockSpec(memory_space=pltpu.VMEM)] * 5,
        out_specs=[pl.BlockSpec(memory_space=pltpu.VMEM)] * 5,
        name="hand_over",
    )(*results)


def solution(mesh):
    split = P(("prefix", "branch"), None, "tensor")
    rows = P(None, "prefix", "tensor")
    ids = P(("prefix", "branch"))
    return jax.shard_map(
        body,
        mesh=mesh,
        in_specs=(split, split, split, split, rows, rows, ids, ids),
        out_specs=(split, split, split, rows, rows),
        check_vma=False,
    )
```

time: 67.2 us -> 65.5 us (0.975)
  Pallas kernels: 64.6 us -> 63.4 us
    pallas_call x1, Pallas kernels: 62.7 us -> 61.4 us  [body(): pl.pallas_call(kernel, out_shape=out_shape, in_specs=[smem, smem] + [hbm]...]
where the time goes in v3:
time: 65.5 us; the launch traced here: 65.3 us
  Pallas kernels  63.4 us (97%)
  between operations  1.93 us (3%)
    pallas_call x1, Pallas kernels, body(): pl.pallas_call(kernel, out_shape=out_shape, in_specs=[smem, smem] + [hbm]...  61.4 us
    pallas_call x1, Pallas kernels, body(): pl.pallas_call(hand_over, out_shape=out_shape, in_specs=[pl.BlockSpec(mem...  1.95 us

profile of v3, /device:TPU:6, one launch (start us, length us, event | category | flops | bytes accessed | tf_op | source)
XLA Modules:
  0.0 65.3 jit_solution(15089521759352369425)
XLA Ops:
  1.9 61.4 %attention_backward.1 = (bf16[1,128,1024]{2,1,0:T(8,128)(2,1)}, bf16[1,128,256]{2,1,0:T(8,128)(2,1)}, bf16[1,128,256]{2,1,0:T(8,128)(2,1)}, bf16[2,128,256]{2,1,0:T(8,128)(2,1)}, bf16[2,128,256]{2,1,0:T(8,128)(2,1)}) custom-call(s32[1]{0:T(128)S(6)} %copy.13.bp_ref, s32[1]{0:T(128)S(6)} %copy.14.bb_ref, bf16[1,128,1024]{2,1,0:T(8,128)(2,1)} %q_hbm.1, ...), custom_call_target="tpu_custom_call" | custom-call | tf_op jit(solution)/shard_map/attention_backward/pallas_call | solution.py:394
  63.3 2.0 %hand_over.1 = (bf16[1,128,1024]{2,1,0:T(8,128)(2,1)}, bf16[1,128,256]{2,1,0:T(8,128)(2,1)}, bf16[1,128,256]{2,1,0:T(8,128)(2,1)}, bf16[2,128,256]{2,1,0:T(8,128)(2,1)}, bf16[2,128,256]{2,1,0:T(8,128)(2,1)}) custom-call(bf16[1,128,1024]{2,1,0:T(8,128)(2,1)} %get-tuple-element.10.refs_0_, bf16[1,128,256]{2,1,0:T(8,128)(2,1)} %get-tuple-element.11.refs_1_, ...), custom_call_target="tpu_custom_call" | custom-call | tf_op jit(solution)/shard_map/hand_over/pallas_call | solution.py:442

commit v4 on v3

v4 whole, which is shorter than its diff:
```python
import math

import jax
import jax.numpy as jnp
from jax import lax
from jax.experimental import pallas as pl
from jax.experimental.pallas import tpu as pltpu
from jax.sharding import PartitionSpec as P

HDIM = 128
BLK = 128
NX = 4
NY = 4
NZ = 8
OWNERS = 2 * NX
GROUP = 4
SCALE = 1.0 / math.sqrt(HDIM)
SCALE2 = SCALE * math.log2(math.e)
MESH = pl.DeviceIdType.MESH

STEPS = (2, 1, 3)
RELS = [(d, dc) for d in STEPS for dc in range(2)] + [(0, 1)]
ROWS = BLK // NY


def nt(a, b):
    return lax.dot_general(a, b, (((1,), (1,)), ((), ())), preferred_element_type=jnp.float32)


def tn(a, b):
    return lax.dot_general(a, b, (((0,), (0,)), ((), ())), preferred_element_type=jnp.float32)


def nn(a, b):
    return lax.dot_general(a, b, (((1,), (0,)), ((), ())), preferred_element_type=jnp.float32)


def fold(a, op):
    return op(a.reshape(a.shape[0] // 8, 8, a.shape[1]), axis=0)


def kernel(
    bp_ref,
    bb_ref,
    q_hbm,
    bk_hbm,
    bv_hbm,
    do_hbm,
    pk_hbm,
    pv_hbm,
    gq_hbm,
    gbk_hbm,
    gbv_hbm,
    fin_hbm,
    q_ref,
    bk_ref,
    bv_ref,
    do_ref,
    gq_ref,
    gbk_ref,
    gbv_ref,
    kva,
    kvb,
    keys,
    qs,
    dos,
    s_buf,
    dp_buf,
    p_buf,
    ds_buf,
    dv_buf,
    own_k,
    own_v,
    term_k,
    term_v,
    got_k,
    got_v,
    acc,
    ys,
    yr,
    zs,
    zr,
    fin,
    a_s,
    a_r,
    b_s,
    b_r,
    u_s,
    u_r,
    ca_s,
    ca_r,
    cb_s,
    cb_r,
    tk_s,
    tk_r,
    tv_s,
    tv_r,
    y_s,
    y_r,
    z_s,
    z_r,
    za_s,
    za_r,
    ya_s,
    ya_r,
    in_s,
    out_s,
):
    me = lax.axis_index("prefix")
    b = lax.axis_index("branch")
    x, c = me // 2, lax.rem(me, 2)
    z, y = b // NY, lax.rem(b, NY)

    def at(dx=0, dc=0, dy=0, dz=0):
        return {
            "prefix": lax.rem(x + dx + NX, NX) * 2 + lax.rem(c + dc, 2),
            "branch": lax.rem(z + dz, NZ) * NY + lax.rem(y + dy + NY, NY),
        }

    def send(src, dst, ss, rs, dev):
        cp = pltpu.make_async_remote_copy(
            src_ref=src, dst_ref=dst, send_sem=ss, recv_sem=rs, device_id=dev, device_id_type=MESH
        )
        cp.start()
        return cp

    def local(src, dst, sem):
        cp = pltpu.make_async_copy(src, dst, sem)
        cp.start()
        return cp

    prefix_in = []
    for g in range(2):
        cols = pl.ds(g * HDIM, HDIM)
        for r in range(NY):
            at_row = pl.multiple_of(lax.rem(y - r + NY, NY) * ROWS, ROWS)
            part = pv_hbm.at[:, pl.ds(at_row, ROWS), cols]
            prefix_in.append(local(part, kvb.at[g, 0, 0, r], in_s.at[(NY + 1) * g + r]))
        prefix_in.append(local(pk_hbm.at[:, :, cols], kva.at[g, 0, 0], in_s.at[(NY + 1) * g + NY]))
    branch_in = [
        local(src, dst, in_s.at[2 * NY + 2 + i])
        for i, (src, dst) in enumerate(
            ((bk_hbm, bk_ref), (bv_hbm, bv_ref), (q_hbm, q_ref), (do_hbm, do_ref))
        )
    ]

    barrier = pltpu.get_barrier_semaphore()
    peers = [at(dx=-d, dc=dc) for d, dc in RELS] + [at(dy=-d, dc=dc) for d, dc in RELS[:-1]]
    peers += [at(dz=d) for d in range(1, NZ)]
    for dev in peers:
        pl.semaphore_signal(barrier, inc=1, device_id=dev, device_id_type=MESH)

    pid = bp_ref[0]
    for cp in prefix_in:
        cp.wait()
    pl.semaphore_wait(barrier, len(peers))

    rest = pl.ds(1, NX - 1)
    ones = range(1, NX)
    first_a, first_b, second_b, over_a, over_b = [], [], [], [], []

    def start_values(g):
        own_v = kvb.at[g, 0, 0, 0]
        first_b.append([send(own_v, kvb.at[g, 0, d, 0], b_s.at[g, d], b_r.at[g, d], at(dx=d)) for d in ones])

    def start_keys(g):
        own_k, own_v = kva.at[g, 0, 0], kvb.at[g, 0, 0]
        first_a.append([send(own_k, kva.at[g, 0, d], a_s.at[g, d], a_r.at[g, d], at(dx=d)) for d in ones])
        over_a.append([send(own_k, kva.at[g, 1, 0], ca_s.at[g, 0], ca_r.at[g, 0], at(dc=1))])
        over_b.append([send(own_v, kvb.at[g, 1, 0], cb_s.at[g, NY], cb_r.at[g, NY], at(dc=1))])

    def pass_keys(g, d):
        first_a[g][d - 1].wait_recv()
        over_a[g].append(send(kva.at[g, 0, d], kva.at[g, 1, d], ca_s.at[g, d], ca_r.at[g, d], at(dc=1)))

    def pass_values(g, d):
        if d:
            second_b[g][d - 1].wait_recv()
        here, there = kvb.at[g, 0, rest, d], kvb.at[g, 1, rest, d]
        over_b[g].append(send(here, there, cb_s.at[g, d], cb_r.at[g, d], at(dc=1)))

    def spread_values(g):
        for cp in first_b[g]:
            cp.wait_recv()
        here = kvb.at[g, 0, rest, 0]
        second_b.append([send(here, kvb.at[g, 0, rest, d], u_s.at[g, d], u_r.at[g, d], at(dy=d)) for d in ones])
        pass_values(g, 0)

    for g in range(2):
        start_values(g)
    for g in range(2):
        start_keys(g)

    for cp in branch_in:
        cp.wait()
    live = lax.broadcasted_iota(jnp.int32, (BLK, HDIM), 0) < bb_ref[0] * BLK
    for g in range(2):
        for h in range(GROUP):
            wide = pl.ds((g * GROUP + h) * HDIM, HDIM)
            qs[g, pl.ds(h * BLK, BLK)] = q_ref[0, :, wide]
            grad = do_ref[0, :, wide]
            dos[g, pl.ds(h * BLK, BLK)] = jnp.where(live, grad, jnp.zeros_like(grad))

    width = GROUP * BLK
    groups = [[], []]

    def own_columns(g):
        return pl.ds(g * HDIM, HDIM)

    def scores(g, slot, count, k, v):
        s = nt(k, qs[g]) * SCALE2
        if slot == OWNERS:
            key = lax.broadcasted_iota(jnp.int32, s.shape, 0)
            query = lax.rem(lax.broadcasted_iota(jnp.int32, s.shape, 1), BLK)
            s = jnp.where(key <= query, s, -1e30)
        s_buf[g, slot : slot + count] = s.reshape(count, BLK, width)
        dp_buf[g, slot : slot + count] = nt(v, dos[g]).reshape(count, BLK, width)
        top = jnp.max(fold(s, jnp.max), axis=0, keepdims=True)
        if groups[g]:
            top = jnp.maximum(top, groups[g][-1][2])

        def exps(i, total):
            e = jnp.exp2(s_buf[g, i] - top)
            s_buf[g, i] = e
            return total + fold(e, jnp.sum)

        total = lax.fori_loop(slot, slot + count, exps, jnp.zeros((8, width), jnp.float32))
        groups[g].append((slot, count, top, total))

    def prefix_scores(g, other, d, count):
        part = pl.ds(d, count)
        ks = [kva[g, other, part, p].reshape(count * BLK, HDIM) for p in range(2)]
        rows = [lax.rem(y - q + NY, NY) for q in range(NY)]
        vs = [
            jnp.concatenate([kvb[g, other, part, r, p][:, None] for r in rows], axis=1)
            .reshape(count * BLK, HDIM)
            for p in range(2)
        ]
        k, v = [jnp.where(pid == 0, pair[0], pair[1]) for pair in (ks, vs)]
        slot = other * NX + d
        keys[g, slot : slot + count] = k.reshape(count, BLK, HDIM)
        scores(g, slot, count, k, v)

    def first_scores(g):
        cols = own_columns(g)
        scores(g, OWNERS, 1, bk_ref[0, :, cols], bv_ref[0, :, cols])
        prefix_scores(g, 0, 0, 1)

    terms_k, terms_v = {}, {}

    def backward(g):
        cols = own_columns(g)
        top = groups[g][-1][2]
        scales = [jnp.exp2(m - top) for _, _, m, _ in groups[g]]
        share = 1.0 / sum(
            jnp.sum(part[3], axis=0, keepdims=True) * scale for part, scale in zip(groups[g], scales)
        )
        total = jnp.zeros((8, width), jnp.float32)
        for (slot, count, _, _), scale in zip(groups[g], scales):
            factor = scale * share

            def probs(i, running):
                low = (s_buf[g, i] * factor).astype(jnp.bfloat16)
                p_buf[g, i] = low
                return running + fold(low.astype(jnp.float32) * dp_buf[g, i], jnp.sum)

            total = lax.fori_loop(slot, slot + count, probs, total)
        delta = jnp.sum(total, axis=0, keepdims=True)
        whose = jnp.full((16, HDIM), pid, jnp.int32).astype(jnp.float32).astype(jnp.bfloat16)
        for k in range(len(RELS)):
            term_k[g, k, BLK : BLK + 16] = whose
            term_v[g, k, BLK : BLK + 16] = whose

        for dc in range(2):
            part = p_buf[g, dc * NX : (dc + 1) * NX].reshape(NX * BLK, width)
            dv_buf[dc] = nn(part, dos[g]).reshape(NX, NY, ROWS, HDIM)
            if dc == 0:
                own_v[g] = dv_buf[dc, :, y].reshape(BLK, HDIM)
            for k, (r, other) in enumerate(RELS):
                if other == dc:
                    there = dv_buf[dc, :, lax.rem(y - r + NY, NY)]
                    term_v[g, k, 0:BLK] = there.reshape(BLK, HDIM).astype(jnp.bfloat16)
                    terms_v[g, k] = send(
                        term_v.at[g, k], got_v.at[g, k], tv_s.at[g, k], tv_r.at[g, k], at(dy=-r, dc=dc)
                    )
        for (slot, count, _, _), scale in zip(groups[g], scales):
            factor = scale * share

            def slopes(i, _):
                p = s_buf[g, i] * factor
                ds_buf[g, i] = (p * (dp_buf[g, i] - delta)).astype(jnp.bfloat16)
                return 0

            lax.fori_loop(slot, slot + count, slopes, 0)
        for dc in range(2):
            part = ds_buf[g, dc * NX : (dc + 1) * NX].reshape(NX * BLK, width)
            dk = (nn(part, qs[g]) * SCALE).reshape(NX, BLK, HDIM)
            if dc == 0:
                own_k[g] = dk[0]
            for k, (d, other) in enumerate(RELS):
                if other == dc:
                    term_k[g, k, 0:BLK] = dk[d].astype(jnp.bfloat16)
                    terms_k[g, k] = send(
                        term_k.at[g, k], got_k.at[g, k], tk_s.at[g, k], tk_r.at[g, k], at(dx=-d, dc=dc)
                    )

    def queries_and_branch(g):
        cols = own_columns(g)
        gbk_ref[0, :, cols] = (nn(ds_buf[g, OWNERS], qs[g]) * SCALE).astype(jnp.bfloat16)
        gbv_ref[0, :, cols] = nn(p_buf[g, OWNERS], dos[g]).astype(jnp.bfloat16)
        dq = tn(keys[g].reshape(OWNERS * BLK, HDIM), ds_buf[g, 0:OWNERS].reshape(OWNERS * BLK, width))
        dq = (dq + tn(bk_ref[0, :, cols], ds_buf[g, OWNERS])) * SCALE
        for h in range(GROUP):
            wide = pl.ds((g * GROUP + h) * HDIM, HDIM)
            gq_ref[0, :, wide] = dq[:, h * BLK : (h + 1) * BLK].T.astype(jnp.bfloat16)

    first_scores(0)
    spread_values(0)
    spread_values(1)
    for d in (1, 3, 2):
        pass_keys(0, d)
    for d in (1, 3, 2):
        pass_values(0, d)
    prefix_scores(0, 0, 1, NX - 1)
    for cp in over_a[0] + over_b[0]:
        cp.wait_recv()
    prefix_scores(0, 1, 0, NX)
    backward(0)
    for d in (1, 3, 2):
        pass_keys(1, d)
    for d in (1, 3, 2):
        pass_values(1, d)
    first_scores(1)
    prefix_scores(1, 0, 1, NX - 1)
    for cp in over_a[1] + over_b[1]:
        cp.wait_recv()
    prefix_scores(1, 1, 0, NX)
    backward(1)
    for g in range(2):
        queries_and_branch(g)
    sent = sum(first_a + first_b + second_b + over_a + over_b, [])
    outs = [
        local(src, dst, out_s.at[i])
        for i, (src, dst) in enumerate(((gq_ref, gq_hbm), (gbk_ref, gbk_hbm), (gbv_ref, gbv_hbm)))
    ]
    sent += list(terms_k.values()) + list(terms_v.values())

    second = {}

    def first_sum(g, kind):
        terms, got, own = ((terms_k, got_k, own_k), (terms_v, got_v, own_v))[kind]
        for k in range(len(RELS)):
            terms[g, k].wait_recv()
        for quarter in range(NY):
            part = pl.ds(quarter * ROWS, ROWS)
            here = own[g, part]
            sums = [jnp.where(pid == p, here, 0.0) for p in range(2)]
            for k in range(len(RELS)):
                t = got[g, k, part].astype(jnp.float32)
                whose = got[g, k, BLK : BLK + 16].astype(jnp.float32)[0:1]
                first = jnp.broadcast_to(whose, t.shape) < 0.5
                sums[0] += jnp.where(first, t, 0.0)
                sums[1] += jnp.where(first, 0.0, t)
            for p in range(2):
                acc[g, kind, quarter, p] = sums[p]
                ys[g, kind, quarter, p] = sums[p].astype(jnp.bfloat16)
        for d in range(1, NY):
            src, dev = (lax.rem(y + d, NY), at(dy=d)) if kind == 0 else (d, at(dx=-d))
            here, there = ys.at[g, kind, src], yr.at[g, kind, d]
            second[g, kind, d] = send(here, there, y_s.at[g, kind, d], y_r.at[g, kind, d], dev)

    for g in range(2):
        first_sum(g, 1)
        first_sum(g, 0)
    sent += second.values()

    along_z = {}
    for g in range(2):
        for kind in (1, 0):
            for d in range(1, NY):
                second[g, kind, d].wait_recv()
            for p in range(2):
                total = acc[g, kind, y if kind == 0 else 0, p]
                for d in range(1, NY):
                    total += yr[g, kind, d, p].astype(jnp.float32)
                zs[g, 4 * p + 2 * kind] = total[0:16]
                zs[g, 4 * p + 2 * kind + 1] = total[16:32]
        for d in range(1, NZ):
            src = zs.at[g, lax.rem(z + d, NZ)]
            along_z[g, d] = send(src, zr.at[g, d], z_s.at[g, d], z_r.at[g, d], at(dz=d))
    sent += along_z.values()

    back_z = {}
    for g in range(2):
        total = zs[g, z]
        for d in range(1, NZ):
            along_z[g, d].wait_recv()
            total += zr[g, d]
        fin[g, y, z] = total.astype(jnp.bfloat16)
        for d in range(1, NZ):
            here = fin.at[g, y, z]
            back_z[g, d] = send(here, here, za_s.at[g, d], za_r.at[g, d], at(dz=d))
    sent += back_z.values()

    back_y = {}
    for g in range(2):
        for d in range(1, NZ):
            back_z[g, d].wait_recv()
        for d in range(1, NY):
            here = fin.at[g, y]
            back_y[g, d] = send(here, here, ya_s.at[g, d], ya_r.at[g, d], at(dy=d))
    sent += back_y.values()

    for cp in back_y.values():
        cp.wait_recv()
    outs.append(local(fin, fin_hbm, out_s.at[3]))
    for cp in sent:
        cp.wait_send()
    for cp in outs:
        cp.wait()


def hand_over(gq_in, gbk_in, gbv_in, fin, gq_ref, gbk_ref, gbv_ref, gpk_ref, gpv_ref):
    gq_ref[...] = gq_in[...]
    gbk_ref[...] = gbk_in[...]
    gbv_ref[...] = gbv_in[...]
    for g in range(2):
        cols = pl.ds(g * HDIM, HDIM)
        for quarter in range(NY):
            for p in range(2):
                for low in range(2):
                    row = pl.ds(quarter * ROWS + low * 16, 16)
                    gpk_ref[p, row, cols] = fin[g, quarter, 4 * p + low]
                    gpv_ref[p, row, cols] = fin[g, quarter, 4 * p + 2 + low]


def body(queries, branch_keys, branch_values, grad_out, prefix_keys, prefix_values, branch_prefix, branch_blocks):
    bf16, f32 = jnp.bfloat16, jnp.float32
    smem = pl.BlockSpec(memory_space=pltpu.SMEM)
    hbm = pl.BlockSpec(memory_space=pltpu.HBM)
    anywhere = pl.BlockSpec(memory_space=pl.ANY)
    width = GROUP * BLK
    dma = pltpu.SemaphoreType.DMA
    shapes = [a.shape for a in (queries, branch_keys, branch_values, prefix_keys, prefix_values)]
    wide, narrow = (pltpu.VMEM(shape, bf16) for shape in shapes[:2])
    out_shape = [jax.ShapeDtypeStruct(shape, bf16) for shape in shapes]
    results = pl.pallas_call(
        kernel,
        out_shape=out_shape[:3] + [jax.ShapeDtypeStruct((2, NY, NZ, 16, HDIM), bf16)],
        in_specs=[smem, smem] + [hbm] * 6,
        out_specs=[anywhere] * 4,
        scratch_shapes=[
            wide,
            narrow,
            narrow,
            wide,
            wide,
            narrow,
            narrow,
            pltpu.VMEM((2, 2, NX, 2, BLK, HDIM), bf16),
            pltpu.VMEM((2, 2, NX, NY, 2, ROWS, HDIM), bf16),
            pltpu.VMEM((2, OWNERS, BLK, HDIM), bf16),
            pltpu.VMEM((2, width, HDIM), bf16),
            pltpu.VMEM((2, width, HDIM), bf16),
            pltpu.VMEM((2, OWNERS + 1, BLK, width), f32),
            pltpu.VMEM((2, OWNERS + 1, BLK, width), f32),
            pltpu.VMEM((2, OWNERS + 1, BLK, width), bf16),
            pltpu.VMEM((2, OWNERS + 1, BLK, width), bf16),
            pltpu.VMEM((2, NX, NY, ROWS, HDIM), f32),
            pltpu.VMEM((2, BLK, HDIM), f32),
            pltpu.VMEM((2, BLK, HDIM), f32),
        ]
        + [pltpu.VMEM((2, len(RELS), BLK + 16, HDIM), bf16)] * 4
        + [
            pltpu.VMEM((2, 2, NY, 2, ROWS, HDIM), f32),
            pltpu.VMEM((2, 2, NY, 2, ROWS, HDIM), bf16),
            pltpu.VMEM((2, 2, NY, 2, ROWS, HDIM), bf16),
            pltpu.VMEM((2, NZ, 16, HDIM), f32),
            pltpu.VMEM((2, NZ, 16, HDIM), f32),
            pltpu.VMEM((2, NY, NZ, 16, HDIM), bf16),
        ]
        + [dma((2, NX))] * 8
        + [dma((2, NY + 1))] * 2
        + [dma((2, len(RELS)))] * 4
        + [dma((2, 2, NY))] * 2
        + [dma((2, NZ))] * 4
        + [dma((2, NY))] * 2
        + [dma((2 * NY + 6,)), dma((4,))],
        compiler_params=pltpu.CompilerParams(
            collective_id=0, has_side_effects=True, vmem_limit_bytes=63 << 20
        ),
        name="attention_backward",
    )(branch_prefix, branch_blocks, queries, branch_keys, branch_values, grad_out, prefix_keys, prefix_values)
    return pl.pallas_call(
        hand_over,
        out_shape=out_shape,
        in_specs=[pl.BlockSpec(memory_space=pltpu.VMEM)] * 4,
        out_specs=[pl.BlockSpec(memory_space=pltpu.VMEM)] * 5,
        name="hand_over",
    )(*results)


def solution(mesh):
    split = P(("prefix", "branch"), None, "tensor")
    rows = P(None, "prefix", "tensor")
    ids = P(("prefix", "branch"))
    return jax.shard_map(
        body,
        mesh=mesh,
        in_specs=(split, split, split, split, rows, rows, ids, ids),
        out_specs=(split, split, split, rows, rows),
        check_vma=False,
    )
```

time: 65.5 us -> 63.5 us (0.969)
  Pallas kernels: 63.4 us -> 61.4 us
    pallas_call x1, Pallas kernels: 61.4 us -> 59.4 us  [body(): pl.pallas_call(kernel, out_shape=out_shape[:3] + [jax.ShapeDtypeStruct((2...]
where the time goes in v4:
time: 63.5 us; the launch traced here: 63.3 us
  Pallas kernels  61.4 us (97%)
  between operations  1.93 us (3%)
    pallas_call x1, Pallas kernels, body(): pl.pallas_call(kernel, out_shape=out_shape[:3] + [jax.ShapeDtypeStruct((2...  59.4 us
    pallas_call x1, Pallas kernels, body(): pl.pallas_call(hand_over, out_shape=out_shape, in_specs=[pl.BlockSpec(mem...  1.96 us

profile of v4, /device:TPU:6, one launch (start us, length us, event | category | flops | bytes accessed | tf_op | source)
XLA Modules:
  0.0 63.3 jit_solution(8374565192393629673)
XLA Ops:
  1.9 59.4 %attention_backward.1 = (bf16[1,128,1024]{2,1,0:T(8,128)(2,1)}, bf16[1,128,256]{2,1,0:T(8,128)(2,1)}, bf16[1,128,256]{2,1,0:T(8,128)(2,1)}, bf16[2,4,8,16,128]{4,3,2,1,0:T(8,128)(2,1)}) custom-call(s32[1]{0:T(128)S(6)} %copy.13.bp_ref, s32[1]{0:T(128)S(6)} %copy.14.bb_ref, bf16[1,128,1024]{2,1,0:T(8,128)(2,1)} %q_hbm.1, bf16[1,128,256]{2,1,0:T(8,128)(2,1)} %bk_hbm.1, ...), custom_call_target="tpu_custom_call" | custom-call | tf_op jit(solution)/shard_map/attention_backward/pallas_call | solution.py:447
  61.3 2.0 %hand_over.1 = (bf16[1,128,1024]{2,1,0:T(8,128)(2,1)}, bf16[1,128,256]{2,1,0:T(8,128)(2,1)}, bf16[1,128,256]{2,1,0:T(8,128)(2,1)}, bf16[2,128,256]{2,1,0:T(8,128)(2,1)}, bf16[2,128,256]{2,1,0:T(8,128)(2,1)}) custom-call(bf16[1,128,1024]{2,1,0:T(8,128)(2,1)} %get-tuple-element.9.gq_in, bf16[1,128,256]{2,1,0:T(8,128)(2,1)} %get-tuple-element.10.gbk_in, ...), custom_call_target="tpu_custom_call" | custom-call | tf_op jit(solution)/shard_map/hand_over/pallas_call | solution.py:494

commit v5 on v4

--- a/solution.py
+++ b/solution.py
@@ -105,6 +105,7 @@
     ya_r,
     in_s,
     out_s,
+    greet,
 ):
     me = lax.axis_index("prefix")
     b = lax.axis_index("branch")
@@ -146,7 +147,8 @@
 
     barrier = pltpu.get_barrier_semaphore()
     peers = [at(dx=-d, dc=dc) for d, dc in RELS] + [at(dy=-d, dc=dc) for d, dc in RELS[:-1]]
-    peers += [at(dz=d) for d in range(1, NZ)]
+    flips = [at(dz=step * (1 - 2 * lax.rem(z // step, 2)) + NZ) for step in (1, 2, 4)]
+    peers += flips
     for dev in peers:
         pl.semaphore_signal(barrier, inc=1, device_id=dev, device_id_type=MESH)
 
@@ -267,9 +269,11 @@
             total = lax.fori_loop(slot, slot + count, probs, total)
         delta = jnp.sum(total, axis=0, keepdims=True)
         whose = jnp.full((16, HDIM), pid, jnp.int32).astype(jnp.float32).astype(jnp.bfloat16)
-        for k in range(len(RELS)):
-            term_k[g, k, BLK : BLK + 16] = whose
-            term_v[g, k, BLK : BLK + 16] = whose
+        if g == 0:
+            for k in range(len(RELS)):
+                term_k[g, k, BLK : BLK + 16] = whose
+                term_v[g, k, BLK : BLK + 16] = whose
+        part_sent = pl.ds(0, BLK + 16 if g == 0 else BLK)
 
         for dc in range(2):
             part = p_buf[g, dc * NX : (dc + 1) * NX].reshape(NX * BLK, width)
@@ -281,7 +285,7 @@
                     there = dv_buf[dc, :, lax.rem(y - r + NY, NY)]
                     term_v[g, k, 0:BLK] = there.reshape(BLK, HDIM).astype(jnp.bfloat16)
                     terms_v[g, k] = send(
-                        term_v.at[g, k], got_v.at[g, k], tv_s.at[g, k], tv_r.at[g, k], at(dy=-r, dc=dc)
+                        term_v.at[g, k, part_sent], got_v.at[g, k, part_sent], tv_s.at[g, k], tv_r.at[g, k], at(dy=-r, dc=dc)
                     )
         for (slot, count, _, _), scale in zip(groups[g], scales):
             factor = scale * share
@@ -301,7 +305,7 @@
                 if other == dc:
                     term_k[g, k, 0:BLK] = dk[d].astype(jnp.bfloat16)
                     terms_k[g, k] = send(
-                        term_k.at[g, k], got_k.at[g, k], tk_s.at[g, k], tk_r.at[g, k], at(dx=-d, dc=dc)
+                        term_k.at[g, k, part_sent], got_k.at[g, k, part_sent], tk_s.at[g, k], tk_r.at[g, k], at(dx=-d, dc=dc)
                     )
 
     def queries_and_branch(g):
@@ -314,8 +318,12 @@
             wide = pl.ds((g * GROUP + h) * HDIM, HDIM)
             gq_ref[0, :, wide] = dq[:, h * BLK : (h + 1) * BLK].T.astype(jnp.bfloat16)
 
-    first_scores(0)
-    spread_values(0)
+    for i in range(2):
+        pl.semaphore_signal(greet.at[i], inc=1, device_id=flips[i], device_id_type=MESH)
+        if i == 0:
+            first_scores(0)
+            spread_values(0)
+            pl.semaphore_wait(greet.at[0], 1)
     spread_values(1)
     for d in (1, 3, 2):
         pass_keys(0, d)
@@ -338,12 +346,12 @@
     backward(1)
     for g in range(2):
         queries_and_branch(g)
-    sent = sum(first_a + first_b + second_b + over_a + over_b, [])
     outs = [
         local(src, dst, out_s.at[i])
         for i, (src, dst) in enumerate(((gq_ref, gq_hbm), (gbk_ref, gbk_hbm), (gbv_ref, gbv_hbm)))
     ]
-    sent += list(terms_k.values()) + list(terms_v.values())
+    for cp in sum(first_a + first_b + second_b + over_a + over_b, []):
+        cp.wait_send()
 
     second = {}
 
@@ -357,7 +365,7 @@
             sums = [jnp.where(pid == p, here, 0.0) for p in range(2)]
             for k in range(len(RELS)):
                 t = got[g, k, part].astype(jnp.float32)
-                whose = got[g, k, BLK : BLK + 16].astype(jnp.float32)[0:1]
+                whose = got[0, k, BLK : BLK + 16].astype(jnp.float32)[0:1]
                 first = jnp.broadcast_to(whose, t.shape) < 0.5
                 sums[0] += jnp.where(first, t, 0.0)
                 sums[1] += jnp.where(first, 0.0, t)
@@ -372,8 +380,10 @@
     for g in range(2):
         first_sum(g, 1)
         first_sum(g, 0)
-    sent += second.values()
-
+    for cp in list(terms_k.values()) + list(terms_v.values()):
+        cp.wait_send()
+
+    pl.semaphore_wait(greet.at[1], 1)
     along_z = {}
     for g in range(2):
         for kind in (1, 0):
@@ -388,36 +398,33 @@
         for d in range(1, NZ):
             src = zs.at[g, lax.rem(z + d, NZ)]
             along_z[g, d] = send(src, zr.at[g, d], z_s.at[g, d], z_r.at[g, d], at(dz=d))
-    sent += along_z.values()
-
-    back_z = {}
+    for cp in second.values():
+        cp.wait_send()
+
     for g in range(2):
         total = zs[g, z]
         for d in range(1, NZ):
             along_z[g, d].wait_recv()
             total += zr[g, d]
-        fin[g, y, z] = total.astype(jnp.bfloat16)
-        for d in range(1, NZ):
-            here = fin.at[g, y, z]
-            back_z[g, d] = send(here, here, za_s.at[g, d], za_r.at[g, d], at(dz=d))
-    sent += back_z.values()
-
-    back_y = {}
-    for g in range(2):
-        for d in range(1, NZ):
-            back_z[g, d].wait_recv()
-        for d in range(1, NY):
-            here = fin.at[g, y]
-            back_y[g, d] = send(here, here, ya_s.at[g, d], ya_r.at[g, d], at(dy=d))
-    sent += back_y.values()
-
-    for cp in back_y.values():
-        cp.wait_recv()
-    outs.append(local(fin, fin_hbm, out_s.at[3]))
-    for cp in sent:
+        fin[y, z, g] = total.astype(jnp.bfloat16)
+    here = fin.at[y, z]
+    back_z = [send(here, here, za_s.at[d], za_r.at[d], at(dz=d)) for d in range(1, NZ)]
+    for cp in along_z.values():
         cp.wait_send()
     for cp in outs:
         cp.wait()
+    for cp in back_z:
+        cp.wait_recv()
+    here = fin.at[y]
+    back_y = [send(here, here, ya_s.at[d], ya_r.at[d], at(dy=d)) for d in range(1, NY)]
+    for cp in back_z:
+        cp.wait_send()
+    for cp in back_y:
+        cp.wait_recv()
+    last = local(fin, fin_hbm, out_s.at[3])
+    for cp in back_y:
+        cp.wait_send()
+    last.wait()
 
 
 def hand_over(gq_in, gbk_in, gbv_in, fin, gq_ref, gbk_ref, gbv_ref, gpk_ref, gpv_ref):
@@ -430,8 +437,8 @@
             for p in range(2):
                 for low in range(2):
                     row = pl.ds(quarter * ROWS + low * 16, 16)
-                    gpk_ref[p, row, cols] = fin[g, quarter, 4 * p + low]
-                    gpv_ref[p, row, cols] = fin[g, quarter, 4 * p + 2 + low]
+                    gpk_ref[p, row, cols] = fin[quarter, 4 * p + low, g]
+                    gpv_ref[p, row, cols] = fin[quarter, 4 * p + 2 + low, g]
 
 
 def body(queries, branch_keys, branch_values, grad_out, prefix_keys, prefix_values, branch_prefix, branch_blocks):
@@ -446,7 +453,7 @@
     out_shape = [jax.ShapeDtypeStruct(shape, bf16) for shape in shapes]
     results = pl.pallas_call(
         kernel,
-        out_shape=out_shape[:3] + [jax.ShapeDtypeStruct((2, NY, NZ, 16, HDIM), bf16)],
+        out_shape=out_shape[:3] + [jax.ShapeDtypeStruct((NY, NZ, 2, 16, HDIM), bf16)],
         in_specs=[smem, smem] + [hbm] * 6,
         out_specs=[anywhere] * 4,
         scratch_shapes=[
@@ -477,15 +484,16 @@
             pltpu.VMEM((2, 2, NY, 2, ROWS, HDIM), bf16),
             pltpu.VMEM((2, NZ, 16, HDIM), f32),
             pltpu.VMEM((2, NZ, 16, HDIM), f32),
-            pltpu.VMEM((2, NY, NZ, 16, HDIM), bf16),
+            pltpu.VMEM((NY, NZ, 2, 16, HDIM), bf16),
         ]
         + [dma((2, NX))] * 8
         + [dma((2, NY + 1))] * 2
         + [dma((2, len(RELS)))] * 4
         + [dma((2, 2, NY))] * 2
-        + [dma((2, NZ))] * 4
-        + [dma((2, NY))] * 2
-        + [dma((2 * NY + 6,)), dma((4,))],
+        + [dma((2, NZ))] * 2
+        + [dma((NZ,))] * 2
+        + [dma((NY,))] * 2
+        + [dma((2 * NY + 6,)), dma((4,)), pltpu.SemaphoreType.REGULAR((2,))],
         compiler_params=pltpu.CompilerParams(
             collective_id=0, has_side_effects=True, vmem_limit_bytes=63 << 20
         ),

time: 63.5 us -> 61.3 us (0.965)
  Pallas kernels: 61.4 us -> 59 us
    pallas_call x1, Pallas kernels: 59.4 us -> 57 us  [body(): pl.pallas_call(kernel, out_shape=out_shape[:3] + [jax.ShapeDtypeStruct((N...]
where the time goes in v5:
time: 61.3 us; the launch traced here: 60.9 us
  Pallas kernels  59 us (96%)
  between operations  1.93 us (3%)
    pallas_call x1, Pallas kernels, body(): pl.pallas_call(kernel, out_shape=out_shape[:3] + [jax.ShapeDtypeStruct((N...  57 us
    pallas_call x1, Pallas kernels, body(): pl.pallas_call(hand_over, out_shape=out_shape, in_specs=[pl.BlockSpec(mem...  1.95 us

profile of v5, /device:TPU:6, one launch (start us, length us, event | category | flops | bytes accessed | tf_op | source)
XLA Modules:
  0.0 60.9 jit_solution(4191007525172424976)
XLA Ops:
  1.9 57.0 %attention_backward.1 = (bf16[1,128,1024]{2,1,0:T(8,128)(2,1)}, bf16[1,128,256]{2,1,0:T(8,128)(2,1)}, bf16[1,128,256]{2,1,0:T(8,128)(2,1)}, bf16[4,8,2,16,128]{4,3,2,1,0:T(8,128)(2,1)}) custom-call(s32[1]{0:T(128)S(6)} %copy.13.bp_ref, s32[1]{0:T(128)S(6)} %copy.14.bb_ref, bf16[1,128,1024]{2,1,0:T(8,128)(2,1)} %q_hbm.1, bf16[1,128,256]{2,1,0:T(8,128)(2,1)} %bk_hbm.1, ...), custom_call_target="tpu_custom_call" | custom-call | tf_op jit(solution)/shard_map/attention_backward/pallas_call | solution.py:454
  58.9 2.0 %hand_over.1 = (bf16[1,128,1024]{2,1,0:T(8,128)(2,1)}, bf16[1,128,256]{2,1,0:T(8,128)(2,1)}, bf16[1,128,256]{2,1,0:T(8,128)(2,1)}, bf16[2,128,256]{2,1,0:T(8,128)(2,1)}, bf16[2,128,256]{2,1,0:T(8,128)(2,1)}) custom-call(bf16[1,128,1024]{2,1,0:T(8,128)(2,1)} %get-tuple-element.9.gq_in, bf16[1,128,256]{2,1,0:T(8,128)(2,1)} %get-tuple-element.10.gbk_in, ...), custom_call_target="tpu_custom_call" | custom-call | tf_op jit(solution)/shard_map/hand_over/pallas_call | solution.py:502

commit v6 on v5

--- a/solution.py
+++ b/solution.py
@@ -153,8 +153,6 @@
         pl.semaphore_signal(barrier, inc=1, device_id=dev, device_id_type=MESH)
 
     pid = bp_ref[0]
-    for cp in prefix_in:
-        cp.wait()
     pl.semaphore_wait(barrier, len(peers))
 
     rest = pl.ds(1, NX - 1)
@@ -162,12 +160,15 @@
     first_a, first_b, second_b, over_a, over_b = [], [], [], [], []
 
     def start_values(g):
-        own_v = kvb.at[g, 0, 0, 0]
+        own_v = pv_hbm.at[:, pl.ds(pl.multiple_of(y * ROWS, ROWS), ROWS), pl.ds(g * HDIM, HDIM)]
         first_b.append([send(own_v, kvb.at[g, 0, d, 0], b_s.at[g, d], b_r.at[g, d], at(dx=d)) for d in ones])
 
     def start_keys(g):
+        own_k = pk_hbm.at[:, :, pl.ds(g * HDIM, HDIM)]
+        first_a.append([send(own_k, kva.at[g, 0, d], a_s.at[g, d], a_r.at[g, d], at(dx=d)) for d in ones])
+
+    def start_over(g):
         own_k, own_v = kva.at[g, 0, 0], kvb.at[g, 0, 0]
-        first_a.append([send(own_k, kva.at[g, 0, d], a_s.at[g, d], a_r.at[g, d], at(dx=d)) for d in ones])
         over_a.append([send(own_k, kva.at[g, 1, 0], ca_s.at[g, 0], ca_r.at[g, 0], at(dc=1))])
         over_b.append([send(own_v, kvb.at[g, 1, 0], cb_s.at[g, NY], cb_r.at[g, NY], at(dc=1))])
 
@@ -192,6 +193,10 @@
         start_values(g)
     for g in range(2):
         start_keys(g)
+    for cp in prefix_in:
+        cp.wait()
+    for g in range(2):
+        start_over(g)
 
     for cp in branch_in:
         cp.wait()

time: 61.3 us -> 61.5 us (level)
  no operation moved by 1% of the time
where the time goes in v6:
time: 61.5 us; the launch traced here: 61.1 us
  Pallas kernels  59.2 us (96%)
  between operations  1.93 us (3%)
    pallas_call x1, Pallas kernels, body(): pl.pallas_call(kernel, out_shape=out_shape[:3] + [jax.ShapeDtypeStruct((N...  57.3 us
    pallas_call x1, Pallas kernels, body(): pl.pallas_call(hand_over, out_shape=out_shape, in_specs=[pl.BlockSpec(mem...  1.95 us

profile of v6, /device:TPU:6, one launch (start us, length us, event | category | flops | bytes accessed | tf_op | source)
XLA Modules:
  0.0 61.1 jit_solution(8922222898357074086)
XLA Ops:
  1.9 57.3 %attention_backward.1 = (bf16[1,128,1024]{2,1,0:T(8,128)(2,1)}, bf16[1,128,256]{2,1,0:T(8,128)(2,1)}, bf16[1,128,256]{2,1,0:T(8,128)(2,1)}, bf16[4,8,2,16,128]{4,3,2,1,0:T(8,128)(2,1)}) custom-call(s32[1]{0:T(128)S(6)} %copy.13.bp_ref, s32[1]{0:T(128)S(6)} %copy.14.bb_ref, bf16[1,128,1024]{2,1,0:T(8,128)(2,1)} %q_hbm.1, bf16[1,128,256]{2,1,0:T(8,128)(2,1)} %bk_hbm.1, ...), custom_call_target="tpu_custom_call" | custom-call | tf_op jit(solution)/shard_map/attention_backward/pallas_call | solution.py:459
  59.2 2.0 %hand_over.1 = (bf16[1,128,1024]{2,1,0:T(8,128)(2,1)}, bf16[1,128,256]{2,1,0:T(8,128)(2,1)}, bf16[1,128,256]{2,1,0:T(8,128)(2,1)}, bf16[2,128,256]{2,1,0:T(8,128)(2,1)}, bf16[2,128,256]{2,1,0:T(8,128)(2,1)}) custom-call(bf16[1,128,1024]{2,1,0:T(8,128)(2,1)} %get-tuple-element.9.gq_in, bf16[1,128,256]{2,1,0:T(8,128)(2,1)} %get-tuple-element.10.gbk_in, ...), custom_call_target="tpu_custom_call" | custom-call | tf_op jit(solution)/shard_map/hand_over/pallas_call | solution.py:507
